TPU v7x, 32 devices: a whole 2x2x4 slice. The times are simulated.
32 devices in a mesh: tm: 4 (over z), row: 8 (over y, x, core).
Axes of the slice: x: 2, y: 2, z: 4, core: 2. Of those that a mesh axis runs over, the one named last changes fastest.
Arguments:
- visible: bfloat16 [4, 8, 8, 4, 1024], P('tm', 'row'), may hold values from -6 to 6
- slot_pos: int32 [4, 8, 8, 4], P('tm', 'row'), may hold values from -1 to 255, as said below
- window_shift: int32 [2, 2], replicated, may hold values from 0 to 3, as said below
- mask_token: bfloat16 [1024], replicated, may hold values from -6 to 6
- w_qkv: bfloat16 [1024, 3072], replicated, may hold values from -6.25 to 6.25
- w_out: bfloat16 [1024, 1024], replicated, may hold values from -0.1875 to 0.1875
- w_head: bfloat16 [1024, 1536], replicated, may hold values from -0.1875 to 0.1875
- pixels: bfloat16 [16, 32, 16, 1536], P('tm', 'row'), may hold values from 0 to 1
Outputs:
- d_visible: bfloat16 [4, 8, 8, 4, 1024], P('tm', 'row')
- d_mask_token: float32 [1024], replicated
Inputs may be any that keep to these rules, and one draw needn't show every extreme that they name: Each live entry slot_pos[i, s, d, c] is a token index of decoder shard (i, d) in frame, row, column order; the live entries aimed at one shard (i, d) are distinct; every slot slot_pos[i, s, s, c] is live, so each shard receives all 4 slots from the packed shard of its own band; other slots are live or -1 at rates that differ from packed shard to packed shard. window_shift[0, g] lies in 0 to 1 and window_shift[1, g] in 0 to 3; some block of columns has row offset 4 - 1 and some block has frame offset 0.
All inputs are finite; a program needn't handle non-finite values.
Results may differ from a plain program's by a relative error of at most 0.014.
Values may be sent and summed in bfloat16 or wider, within the bound.
A program may use at most 128 MiB of HBM per device.

v0:
```python
import math

import jax
import jax.numpy as jnp
from jax import lax
from jax.sharding import PartitionSpec as P

HEADS = 16
WT = 2
WH = 4
WW = 8


def from_behind(value, axis, steps):
    count = lax.axis_size(axis)
    pairs = [(source, (source + steps) % count) for source in range(count)]
    return lax.ppermute(value, axis, pairs)


def as_sent(shard):
    return jax.tree.map(lambda a: a.astype(jnp.bfloat16) if a.dtype == jnp.float32 else a, shard)


def layer_norm(values):
    center = values - jnp.mean(values, axis=-1, keepdims=True)
    return center * lax.rsqrt(jnp.mean(center * center, axis=-1, keepdims=True) + 1e-05)


def sinusoid(coordinate, channel_count):
    half_count = channel_count // 2
    frequency = jnp.exp(-math.log(10000.0) * jnp.arange(half_count, dtype=jnp.float32) / half_count)
    angles = coordinate.astype(jnp.float32)[..., None] * frequency
    return jnp.concatenate([jnp.sin(angles), jnp.cos(angles)], axis=-1)


def position_table(frame_pos, row_pos, column_pos, model_width):
    quarter = model_width // 4
    remainder = (model_width - quarter) // 2
    return jnp.concatenate(
        [
            sinusoid(frame_pos, quarter),
            sinusoid(row_pos, remainder),
            sinusoid(column_pos, model_width - quarter - remainder),
        ],
        axis=-1,
    )


def window_core(grid_block, w_qkv, w_out):
    frame_count, row_count, column_count, model_width = grid_block.shape
    head_dim = model_width // HEADS
    normed = layer_norm(grid_block).astype(jnp.bfloat16)
    packed = jnp.dot(
        normed.reshape(-1, model_width), w_qkv, preferred_element_type=jnp.float32
    ).astype(jnp.bfloat16)
    packed = packed.reshape(
        frame_count // WT, WT, row_count // WH, WH, column_count // WW, WW, 3, HEADS, head_dim
    )
    packed = packed.transpose(6, 0, 2, 4, 7, 1, 3, 5, 8).reshape(
        3, -1, HEADS, WT * WH * WW, head_dim
    )
    scores = jnp.einsum(
        "nhqe,nhke->nhqk", packed[0], packed[1], preferred_element_type=jnp.float32
    ) * head_dim ** (-0.5)
    weights = jax.nn.softmax(scores, axis=-1).astype(jnp.bfloat16)
    mixed_heads = jnp.einsum(
        "nhqk,nhke->nhqe", weights, packed[2], preferred_element_type=jnp.float32
    ).astype(jnp.bfloat16)
    mixed_heads = mixed_heads.reshape(
        frame_count // WT, row_count // WH, column_count // WW, HEADS, WT, WH, WW, head_dim
    )
    mixed_heads = mixed_heads.transpose(0, 4, 1, 5, 2, 6, 3, 7).reshape(-1, model_width)
    result_rows = jnp.dot(mixed_heads, w_out, preferred_element_type=jnp.float32)
    return result_rows.reshape(frame_count, row_count, column_count, model_width)


def pixel_gradient(stream_rows, pixel_rows, masked, w_head):
    row_total, pixel_count = pixel_rows.shape
    group_size = pixel_count // 3
    raw_pixels = pixel_rows.astype(jnp.float32).reshape(row_total, 3, group_size)
    center = raw_pixels - jnp.mean(raw_pixels, axis=-1, keepdims=True)
    spread = jnp.sqrt(jnp.sum(center * center, axis=-1, keepdims=True) / (group_size - 1))
    target = (center / (spread + 1e-06)).reshape(row_total, pixel_count)

    def pixel_loss(values):
        normed = layer_norm(values).astype(jnp.bfloat16)
        predicted = jnp.dot(normed, w_head, preferred_element_type=jnp.float32)
        errors = predicted - target
        return 0.5 * jnp.sum(masked[:, None] * errors * errors)

    return jax.grad(pixel_loss)(stream_rows)


def regroup(joined, offsets, base, length, axis, sign):
    pieces = []
    for group in range(offsets.shape[0]):
        piece = joined[:, :, group * WW : (group + 1) * WW]
        pieces.append(lax.dynamic_slice_in_dim(piece, base + sign * offsets[group], length, axis))
    return jnp.concatenate(pieces, axis=2)


def align_block(grid_block, time_offsets, row_offsets):
    rim_time = WT - 1
    rim_row = WH - 1
    frame_count = grid_block.shape[0]
    row_count = grid_block.shape[1]
    lower_frames = from_behind(grid_block[frame_count - rim_time :], "tm", 1)
    joined = jnp.concatenate([lower_frames, grid_block], axis=0)
    grid_block = regroup(joined, time_offsets, rim_time, frame_count, 0, -1)
    lower_rows = from_behind(grid_block[:, row_count - rim_row :], "row", 1)
    joined = jnp.concatenate([lower_rows, grid_block], axis=1)
    return regroup(joined, row_offsets, rim_row, row_count, 1, -1)


def return_values(aligned, time_offsets, row_offsets):
    rim_time = WT - 1
    rim_row = WH - 1
    frame_count = aligned.shape[0]
    row_count = aligned.shape[1]
    upper_rows = from_behind(aligned[:, :rim_row], "row", -1)
    joined = jnp.concatenate([aligned, upper_rows], axis=1)
    aligned = regroup(joined, row_offsets, 0, row_count, 1, 1)
    upper_frames = from_behind(aligned[:rim_time], "tm", -1)
    joined = jnp.concatenate([aligned, upper_frames], axis=0)
    return regroup(joined, time_offsets, 0, frame_count, 0, 1)


def return_grads(aligned, time_offsets, row_offsets):
    rim_time = WT - 1
    rim_row = WH - 1
    frame_count = aligned.shape[0]
    row_count = aligned.shape[1]
    upper_rows = from_behind(aligned[:, :rim_row].astype(jnp.bfloat16), "row", -1).astype(
        jnp.float32
    )
    joined = jnp.concatenate([aligned, upper_rows], axis=1)
    aligned = regroup(joined, row_offsets, 0, row_count, 1, 1)
    upper_frames = from_behind(as_sent(aligned[:rim_time]), "tm", -1)
    joined = jnp.concatenate([aligned, upper_frames], axis=0)
    return regroup(joined, time_offsets, 0, frame_count, 0, 1)


def per_device(visible, slot_pos, window_shift, mask_token, w_qkv, w_out, w_head, pixels):
    frame_count, row_count, column_count, pixel_count = pixels.shape
    model_width = mask_token.shape[0]
    tokens = frame_count * row_count * column_count
    peer_count = slot_pos.shape[2]
    slot_count = slot_pos.shape[3]
    sent_rows = visible.reshape(peer_count, slot_count, model_width)
    sent_index = slot_pos.reshape(peer_count, slot_count)
    got_rows, got_index = (
        lax.all_to_all(sent_rows, "row", split_axis=0, concat_axis=0, tiled=True),
        lax.all_to_all(sent_index, "row", split_axis=0, concat_axis=0, tiled=True),
    )
    flat_index = got_index.reshape(-1)
    is_live = flat_index >= 0
    target_index = jnp.where(is_live, flat_index, tokens).astype(jnp.int32)
    visible_grid = (
        jnp.zeros((tokens, model_width), jnp.float32)
        .at[target_index]
        .set(got_rows.reshape(-1, model_width).astype(jnp.float32), mode="drop")
    )
    seen_flags = jnp.zeros((tokens,), jnp.float32).at[target_index].set(1.0, mode="drop")
    local_index = jnp.arange(tokens, dtype=jnp.int32)
    frame_global = lax.axis_index("tm") * frame_count + local_index // (row_count * column_count)
    row_global = lax.axis_index("row") * row_count + local_index // column_count % row_count
    position_rows = position_table(
        frame_global, row_global, local_index % column_count, model_width
    )
    start_rows = jnp.where(
        seen_flags[:, None] > 0, visible_grid, mask_token.astype(jnp.float32)[None, :]
    )
    embedded = (
        (start_rows + position_rows)
        .astype(jnp.bfloat16)
        .reshape(frame_count, row_count, column_count, model_width)
    )
    stream = embedded.astype(jnp.float32)
    time_offsets = window_shift[0]
    row_offsets = window_shift[1]

    def core_only(grid_block):
        return window_core(grid_block, w_qkv, w_out)

    aligned = align_block(embedded, time_offsets, row_offsets)
    attn_aligned, pull_back = jax.vjp(core_only, aligned.astype(jnp.float32))
    attn_value = return_values(attn_aligned.astype(jnp.bfloat16), time_offsets, row_offsets)
    residual = stream + attn_value.astype(jnp.float32)
    masked = 1.0 - seen_flags
    grad_stream = pixel_gradient(
        residual.reshape(tokens, model_width), pixels.reshape(tokens, pixel_count), masked, w_head
    )
    grad_attn = lax.optimization_barrier(grad_stream.astype(jnp.bfloat16)).reshape(
        frame_count, row_count, column_count, model_width
    )
    grad_in = align_block(grad_attn, time_offsets, row_offsets).astype(jnp.float32)
    grad_aligned = pull_back(grad_in)[0]
    grad_core = return_grads(grad_aligned, time_offsets, row_offsets)
    grad_embedded = grad_stream + grad_core.reshape(tokens, model_width)
    picked = grad_embedded[jnp.minimum(target_index, tokens - 1)] * is_live[:, None].astype(
        jnp.float32
    )
    picked = picked.astype(jnp.bfloat16).reshape(peer_count, slot_count, model_width)
    returned = lax.all_to_all(picked, "row", split_axis=0, concat_axis=0, tiled=True)
    d_visible = returned.reshape(visible.shape)
    local_total = jnp.sum(masked[:, None] * grad_embedded, axis=0)
    mask_total = lax.psum(local_total, ("tm", "row"))
    grad_scale = (tokens * lax.axis_size("tm") * lax.axis_size("row")) ** (-0.5)
    return (d_visible, mask_total * grad_scale)


def solution(mesh):
    placed = (
        P("tm", "row", None, None, None),
        P("tm", "row", None, None),
        P(),
        P(),
        P(),
        P(),
        P(),
        P("tm", "row", None, None),
    )
    return jax.shard_map(
        per_device,
        mesh=mesh,
        in_specs=placed,
        out_specs=(P("tm", "row", None, None, None), P()),
        check_vma=False,
    )
```

profile of v0, /device:TPU:0, one launch (start us, length us, event | category | flops | bytes accessed | tf_op | source)
XLA Modules:
  0.0 225.7 jit_solution(14510782064491890069)
XLA Ops:
  0.6 1.5 copy.47
  2.1 5.2 %all-to-all-start = ((s32[8,1,4]{2,1,0:T(1,128)}), s32[8,1,4]{2,1,0:T(1,128)S(1)}, u32[]{:S(2)}, u32[]{:S(2)}) async-start(s32[8,1,4]{2,1,0:T(1,128)} %copy.47), calls=%async_computation | async-start | bytes 8192 | tf_op jit(solution)/shard_map/all_to_all | solution.py:153
  8.6 3.8 %reshape.338 = f32[256,3,512]{2,1,0:T(4,128)} reshape(bf16[4,4,16,1536]{3,2,1,0:T(8,128)(2,1)} %param.15) | data formatting | bytes 2359296 | tf_op jit(solution)/shard_map/convert_element_type | solution.py:80
  12.4 2.0 reduce_sum.144
  14.3 1.2 multiply_cosine_fusion.2
  15.6 3.6 %multiply_cosine_fusion = (f32[256,192]{1,0:T(8,128)S(1)}, f32[256,192]{1,0:T(8,128)}, f32[256,192]{1,0:T(8,128)}, f32[256,192]{1,0:T(8,128)}) fusion(f32[256]{0:T(256)S(1)} %get-tuple-element.43, f32[192]{0:T(256)} %multiply_exponential_fusion, f32[256]{0:T(256)S(1)} %get-tuple-element.44), kind=kLoop, calls=%fused_computation.97 | loop fusion | flops 98304 | bytes 789248 | tf_op jit(solution)/shard_map/cos | solution.py:33
  19.2 2.2 concatenate.51
  21.4 4.2 %all-to-all-start.1 = ((bf16[8,4,1024]{2,1,0:T(4,128)(2,1)}), bf16[8,4,1024]{2,1,0:T(4,128)(2,1)S(1)}, u32[]{:S(2)}, u32[]{:S(2)}) async-start(bf16[8,4,1024]{2,1,0:T(4,128)(2,1)} %bitcast.123), calls=%async_computation.1 | async-start | bytes 131072 | tf_op jit(solution)/shard_map/all_to_all | solution.py:152
  28.1 2.5 %all-to-all-done.1 = bf16[8,4,1024]{2,1,0:T(4,128)(2,1)S(1)} async-done(((bf16[8,4,1024]{2,1,0:T(4,128)(2,1)}), bf16[8,4,1024]{2,1,0:T(4,128)(2,1)S(1)}, u32[]{:S(2)}, u32[]{:S(2)}) %all-to-all-start.1) | async-done | bytes 65568 | tf_op jit(solution)/shard_map/all_to_all | solution.py:152
  30.6 1.7 scatter_custom_fusion.1
  32.3 1.7 add_convert_fusion
  34.8 1.6 collective-permute-start
  44.0 1.5 multiply_reduce_fusion
  46.5 1.3 div.139
  47.8 3.0 %copy.56 = f32[256,1536]{1,0:T(8,128)} copy(f32[256,1536]{0,1:T(8,128)} %bitcast.104) | data formatting | bytes 3145728 | tf_op jit(solution)/shard_map/div | solution.py:83
  50.9 1.3 sub.75.clone
  52.1 3.1 %copy.54 = f32[256,1536]{1,0:T(8,128)} copy(f32[256,1536]{0,1:T(8,128)} %bitcast.105) | data formatting | bytes 3145728 | tf_op jit(solution)/shard_map/sub | solution.py:81
  57.5 1.2 multiply_reduce_fusion.5
  60.0 5.8 %convolution_convert_fusion = bf16[256,3072]{1,0:T(8,128)(2,1)} fusion(bf16[256,1024]{1,0:T(8,128)(2,1)S(1)} %multiply_convert_fusion.1, bf16[1024,3072]{1,0:T(8,128)(2,1)} %param.12), kind=kOutput, calls=%fused_computation.4 | convolution fusion | flops 1611399168 | bytes 8388608 | tf_op jit(solution)/shard_map/jvp()/dot_general | solution.py:53
  65.8 4.9 %reshape.324 = bf16[2,2,1,4,2,8,3,16,64]{8,7,6,5,4,3,1,0,2:T(8,128)(2,1)} reshape(bf16[256,3072]{1,0:T(8,128)(2,1)} %convolution_convert_fusion) | data formatting | bytes 3145728 | tf_op jit(solution)/shard_map/jvp()/reshape | solution.py:56
  70.7 2.7 %fusion.66 = (bf16[1,2,1,2,16,2,4,8,64]{8,4,0,7,3,6,5,1,2:T(8,128)(2,1)S(1)}, bf16[1,2,1,2,16,2,4,8,64]{8,4,0,7,3,6,5,1,2:T(8,128)(2,1)S(1)}, bf16[1,2,1,2,16,2,4,8,64]{8,4,0,7,3,6,5,1,2:T(8,128)(2,1)S(1)}) fusion(bf16[3,2,1,2,16,2,4,8,64]{8,4,0,7,3,6,5,1,2:T(8,128)(2,1)} %bitcast.100), kind=kLoop, calls=%fused_computation.177 | loop fusion | bytes 3145728 | tf_op jit(solution)/shard_map/jvp()/slice | solution.py:67
  73.4 1.3 copy.50
  74.7 1.3 copy.49
  75.9 1.3 copy.48
  77.2 3.7 %fusion.72 = (f32[4,16,64]{2,1,0:T(8,128)S(1)}, f32[4,16,64,64]{2,3,1,0:T(8,128)}) fusion(bf16[4,16,64,64]{3,2,1,0:T(8,128)(2,1)} %bitcast.116, bf16[4,16,64,64]{3,2,1,0:T(8,128)(2,1)} %bitcast.114), kind=kOutput, calls=%fused_computation.183 | convolution fusion | flops 34340928 | bytes 2113536 | tf_op jit(solution)/shard_map/jvp()/sub | solution.py:65
  80.9 2.4 %convolution_convert_fusion.5 = bf16[4,16,64,64]{3,2,1,0:T(8,128)(2,1)S(1)} fusion(bf16[4,16,64,64]{3,2,1,0:T(8,128)(2,1)} %bitcast.109, f32[4,16,64,64]{2,3,1,0:T(8,128)} %get-tuple-element.36, f32[4,16,64]{2,1,0:T(8,128)S(1)} %get-tuple-element.35), kind=kOutput, calls=%fused_computation.38 | convolution fusion | flops 34340864 | bytes 2113536 | tf_op jit(solution)/shard_map/jvp(nhqk,nhke->nhqe)/dot_general | solution.py:66
  83.2 2.2 copy.52
  85.4 2.6 %dot_general.41 = bf16[4,4,16,1024]{3,2,1,0:T(8,128)(2,1)} reshape(bf16[2,2,1,4,2,8,16,64]{7,6,5,4,3,1,0,2:T(8,128)(2,1)} %copy.52) | data formatting | bytes 1048576 | tf_op jit(solution)/shard_map/jvp()/dot_general | solution.py:73
  88.0 2.6 %fusion.22 = bf16[4,4,16,1024]{3,2,1,0:T(8,128)(2,1)S(1)} fusion(bf16[4,4,16,1024]{3,2,1,0:T(8,128)(2,1)} %dot_general.41, bf16[1024,1024]{1,0:T(8,128)(2,1)} %param.13), kind=kOutput, calls=%fused_computation.48 | convolution fusion | flops 537133056 | bytes 3145728 | tf_op jit(solution)/shard_map/jvp()/dot_general | solution.py:73
  92.2 2.6 %collective-permute-start.2 = (bf16[4,3,16,1024]{3,2,1,0:T(8,128)(2,1)}, bf16[4,3,16,1024]{3,2,1,0:T(8,128)(2,1)}, u32[]{:S(2)}, u32[]{:S(2)}) collective-permute-start(bf16[4,3,16,1024]{3,2,1,0:T(8,128)(2,1)} %slice.169), channel_id=1, source_target_pairs={{0,7},{1,0},{2,1},{3,2},{4,3},{5,4},{6,5},{7,6},{8,15},{9,8},{10,9... | collective-permute-start | bytes 1179656 | tf_op jit(solution)/shard_map/ppermute | solution.py:17
  94.9 1.5 fusion.9
  107.0 2.0 collective-permute-start.3
  109.0 3.2 %collective-permute-done.3 = bf16[1,4,16,1024]{3,2,1,0:T(8,128)(2,1)S(1)} collective-permute-done((bf16[1,4,16,1024]{3,2,1,0:T(8,128)(2,1)S(1)}, bf16[1,4,16,1024]{3,2,1,0:T(8,128)(2,1)S(1)}, u32[]{:S(2)}, u32[]{:S(2)}) %collective-permute-start.3) | collective-permute-done | bytes 131104 | tf_op jit(solution)/shard_map/ppermute | solution.py:17
  113.3 4.7 %fusion.25 = (f32[256]{0:T(256)S(1)}, bf16[256,1024]{1,0:T(8,128)(2,1)}) fusion(bf16[256,1024]{1,0:T(8,128)(2,1)} %copy-done.2, bf16[4,4,16,1024]{3,2,1,0:T(8,128)(2,1)} %copy-done.10, f32[256]{0:T(256)S(1)} %broadcast_multiply_fusion.4, bf16[1024,1536]{1,0:T(8,128)(2,1)S(1)} %copy-done, f32[256]{0:T(256)S(1)} %get-tuple-element.25, ...), kind=kOutput, calls=%fused_computation.50 | convolution fusion | flops 1616248576 | bytes 6820864 | tf_op jit(solution)/shard_map/transpose(jvp())/dot_general | solution.py:87
  118.0 1.8 fusion.65
  120.7 6.1 %collective-permute-done.4 = bf16[1,4,16,1024]{3,2,1,0:T(8,128)(2,1)S(1)} collective-permute-done((bf16[1,4,16,1024]{3,2,1,0:T(8,128)(2,1)S(1)}, bf16[1,4,16,1024]{3,2,1,0:T(8,128)(2,1)S(1)}, u32[]{:S(2)}, u32[]{:S(2)}) %collective-permute-start.4) | collective-permute-done | bytes 131104 | tf_op jit(solution)/shard_map/ppermute | solution.py:17
  127.1 8.1 %collective-permute-done.5 = bf16[4,3,16,1024]{3,2,1,0:T(8,128)(2,1)S(1)} collective-permute-done((bf16[4,3,16,1024]{3,2,1,0:T(8,128)(2,1)S(1)}, bf16[4,3,16,1024]{3,2,1,0:T(8,128)(2,1)S(1)}, u32[]{:S(2)}, u32[]{:S(2)}) %collective-permute-start.5) | collective-permute-done | bytes 393248 | tf_op jit(solution)/shard_map/ppermute | solution.py:17
  135.4 1.4 copy-done.24
  144.3 5.3 %copy.67 = bf16[3,2,1,2,16,2,4,8,64]{8,4,0,7,3,6,5,1,2:T(8,128)(2,1)} copy(bf16[3,2,1,2,16,2,4,8,64]{8,7,6,5,4,3,1,0,2:T(8,128)(2,1)S(1)} %bitcast.101) | data formatting | bytes 3145728 | tf_op jit(solution)/shard_map/transpose(jvp())/reshape | solution.py:59
  149.6 5.0 %reshape.331 = bf16[256,3072]{1,0:T(8,128)(2,1)} reshape(bf16[2,2,1,4,2,8,3,16,64]{8,7,6,5,4,3,1,0,2:T(8,128)(2,1)} %bitcast.102) | data formatting | bytes 3145728 | tf_op jit(solution)/shard_map/transpose(jvp())/reshape | solution.py:56
  154.6 5.2 %multiply_reduce_fusion.3 = (f32[256]{0:T(256)S(1)}, f32[256,1024]{1,0:T(8,128)S(1)}) fusion(f32[256]{0:T(256)S(1)} %div.129, bf16[4,4,8,1024]{3,2,1,0:T(8,128)(2,1)S(1)} %copy-done.9, bf16[4,4,8,1024]{3,2,1,0:T(8,128)(2,1)S(1)} %constant_dynamic-slice_fusion.7, bf16[256,3072]{1,0:T(8,128)(2,1)} %reshape.331, bf16[1024,3072]{1,0:T(8,128)(2,1)} %param.12), kind=kOutput, calls=%fused_computation.58 | convolution fusion | flops 1612971776 | bytes 9439232 | tf_op jit(solution)/shard_map/transpose(jvp())/dot_general | solution.py:53
  161.0 5.1 %collective-permute-done.6 = bf16[4,3,16,1024]{3,2,1,0:T(8,128)(2,1)S(1)} collective-permute-done((bf16[4,3,16,1024]{3,2,1,0:T(8,128)(2,1)S(1)}, bf16[4,3,16,1024]{3,2,1,0:T(8,128)(2,1)S(1)}, u32[]{:S(2)}, u32[]{:S(2)}) %collective-permute-start.6) | collective-permute-done | bytes 393248 | tf_op jit(solution)/shard_map/ppermute | solution.py:17
  166.6 1.8 collective-permute-start.7
  168.4 3.1 %collective-permute-done.7 = bf16[1,4,16,1024]{3,2,1,0:T(8,128)(2,1)S(1)} collective-permute-done((bf16[1,4,16,1024]{3,2,1,0:T(8,128)(2,1)S(1)}, bf16[1,4,16,1024]{3,2,1,0:T(8,128)(2,1)S(1)}, u32[]{:S(2)}, u32[]{:S(2)}) %collective-permute-start.7) | collective-permute-done | bytes 131104 | tf_op jit(solution)/shard_map/ppermute | solution.py:17
  174.3 38.9 %psum.7 = f32[1024]{0:T(1024)S(1)} all-reduce(f32[1024]{0:T(1024)S(1)} %get-tuple-element.2), channel_id=1, replica_groups=mesh['tm'=4,'row'=8] {'tm','row'}, use_global_device_ids=true, to_apply=%region_16.17 | all-reduce | flops 1024 | bytes 8192 | tf_op jit(solution)/shard_map/psum | solution.py:207
  213.1 1.9 gather_fusion
  215.8 4.3 %all-to-all-start.2 = ((bf16[8,4,1024]{2,1,0:T(4,128)(2,1)}), bf16[8,4,1024]{2,1,0:T(4,128)(2,1)S(1)}, u32[]{:S(2)}, u32[]{:S(2)}) async-start(bf16[8,4,1024]{2,1,0:T(4,128)(2,1)} %multiply_convert_fusion.4), calls=%async_computation.2 | async-start | bytes 131072 | tf_op jit(solution)/shard_map/all_to_all | solution.py:204
  220.7 4.4 %all-to-all-done.2 = bf16[8,4,1024]{2,1,0:T(4,128)(2,1)S(1)} async-done(((bf16[8,4,1024]{2,1,0:T(4,128)(2,1)}), bf16[8,4,1024]{2,1,0:T(4,128)(2,1)S(1)}, u32[]{:S(2)}, u32[]{:S(2)}) %all-to-all-start.2) | async-done | bytes 65568 | tf_op jit(solution)/shard_map/all_to_all | solution.py:204
  (161 shorter events, 34.7 us)
Async XLA Ops:
  0.6 112.6 %copy-start = (bf16[1024,1536]{1,0:T(8,128)(2,1)S(1)}, bf16[1024,1536]{1,0:T(8,128)(2,1)}, u32[]{:S(2)}) copy-start(bf16[1024,1536]{1,0:T(8,128)(2,1)} %param.14) | copy-start | bytes 9437188
  2.1 19.3 %all-to-all-start = ((s32[8,1,4]{2,1,0:T(1,128)}), s32[8,1,4]{2,1,0:T(1,128)S(1)}, u32[]{:S(2)}, u32[]{:S(2)}) async-start(s32[8,1,4]{2,1,0:T(1,128)} %copy.47), calls=%async_computation | async-start | bytes 8192 | tf_op jit(solution)/shard_map/all_to_all | solution.py:153
  21.4 9.2 %all-to-all-start.1 = ((bf16[8,4,1024]{2,1,0:T(4,128)(2,1)}), bf16[8,4,1024]{2,1,0:T(4,128)(2,1)S(1)}, u32[]{:S(2)}, u32[]{:S(2)}) async-start(bf16[8,4,1024]{2,1,0:T(4,128)(2,1)} %bitcast.123), calls=%async_computation.1 | async-start | bytes 131072 | tf_op jit(solution)/shard_map/all_to_all | solution.py:152
  25.6 10.9 %copy-start.22 = (s32[2,2]{1,0:T(2,128)S(1)}, s32[2,2]{1,0:T(2,128)}, u32[]{:S(2)}) copy-start(s32[2,2]{1,0:T(2,128)} %param.10) | copy-start | bytes 52
  34.0 0.8 copy-start.2
  34.8 7.0 %collective-permute-start = (bf16[1,4,16,1024]{3,2,1,0:T(8,128)(2,1)S(1)}, bf16[1,4,16,1024]{3,2,1,0:T(8,128)(2,1)S(1)}, u32[]{:S(2)}, u32[]{:S(2)}) collective-permute-start(bf16[1,4,16,1024]{3,2,1,0:T(8,128)(2,1)S(1)} %bitcast.121), channel_id=1, source_target_pairs={{0,8},{8,16},{16,24},{24,0},{1,9},{9,17},{17,25},{25,1},{2,10},{10... | collective-permute-start | bytes 393224 | tf_op jit(solution)/shard_map/ppermute | solution.py:17
  39.7 2.8 %copy-start.3 = (bf16[256,1024]{1,0:T(8,128)(2,1)S(1)}, bf16[256,1024]{1,0:T(8,128)(2,1)}, u32[]{:S(2)}) copy-start(bf16[256,1024]{1,0:T(8,128)(2,1)} %copy-done.2) | copy-start | bytes 1572868
  39.7 4.3 %copy-start.5 = (f32[256,3,512]{2,1,0:T(4,128)S(1)}, f32[256,3,512]{2,1,0:T(4,128)}, u32[]{:S(2)}) copy-start(f32[256,3,512]{2,1,0:T(4,128)} %reshape.338) | copy-start | bytes 4718596
  41.8 0.7 copy-start.21
  42.5 0.7 copy-start.17
  44.0 11.2 %collective-permute-start.1 = (bf16[4,3,16,1024]{3,2,1,0:T(8,128)(2,1)}, bf16[4,3,16,1024]{3,2,1,0:T(8,128)(2,1)}, u32[]{:S(2)}, u32[]{:S(2)}) collective-permute-start(bf16[4,3,16,1024]{3,2,1,0:T(8,128)(2,1)} %pad_maximum_fusion.7), channel_id=1, source_target_pairs={{0,1},{1,2},{2,3},{3,4},{4,5},{5,6},{6,7},{7,0},{8,9},{9,10},{10,1... | collective-permute-start | bytes 1179656 | tf_op jit(solution)/shard_map/ppermute | solution.py:17
  56.5 0.7 copy-start.8
  88.0 6.8 %copy-start.11 = (f32[256,1536]{1,0:T(8,128)S(1)}, f32[256,1536]{1,0:T(8,128)}, u32[]{:S(2)}) copy-start(f32[256,1536]{1,0:T(8,128)} %copy.56) | copy-start | bytes 4718596
  88.0 6.8 %copy-start.12 = (f32[256,1536]{1,0:T(8,128)S(1)}, f32[256,1536]{1,0:T(8,128)}, u32[]{:S(2)}) copy-start(f32[256,1536]{1,0:T(8,128)} %copy.54) | copy-start | bytes 4718596
  88.0 6.8 %copy-start.16 = (bf16[4,4,16,1536]{3,2,1,0:T(8,128)(2,1)S(1)}, bf16[4,4,16,1536]{3,2,1,0:T(8,128)(2,1)}, u32[]{:S(2)}) copy-start(bf16[4,4,16,1536]{3,2,1,0:T(8,128)(2,1)} %param.15) | copy-start | bytes 2359300
  90.6 0.8 copy-start.14
  92.2 12.7 %collective-permute-start.2 = (bf16[4,3,16,1024]{3,2,1,0:T(8,128)(2,1)}, bf16[4,3,16,1024]{3,2,1,0:T(8,128)(2,1)}, u32[]{:S(2)}, u32[]{:S(2)}) collective-permute-start(bf16[4,3,16,1024]{3,2,1,0:T(8,128)(2,1)} %slice.169), channel_id=1, source_target_pairs={{0,7},{1,0},{2,1},{3,2},{4,3},{5,4},{6,5},{7,6},{8,15},{9,8},{10,9... | collective-permute-start | bytes 1179656 | tf_op jit(solution)/shard_map/ppermute | solution.py:17
  103.8 2.1 copy-start.15
  107.0 5.2 %collective-permute-start.3 = (bf16[1,4,16,1024]{3,2,1,0:T(8,128)(2,1)S(1)}, bf16[1,4,16,1024]{3,2,1,0:T(8,128)(2,1)S(1)}, u32[]{:S(2)}, u32[]{:S(2)}) collective-permute-start(bf16[1,4,16,1024]{3,2,1,0:T(8,128)(2,1)S(1)} %pad_maximum_fusion.9), channel_id=1, source_target_pairs={{0,24},{8,0},{16,8},{24,16},{1,25},{9,1},{17,9},{25,17},{2,26},{10... | collective-permute-start | bytes 393224 | tf_op jit(solution)/shard_map/ppermute | solution.py:17
  109.0 3.5 %copy-start.4 = (bf16[256,1024]{1,0:T(8,128)(2,1)S(1)}, bf16[256,1024]{1,0:T(8,128)(2,1)}, u32[]{:S(2)}) copy-start(bf16[256,1024]{1,0:T(8,128)(2,1)} %copy-done.2) | copy-start | bytes 1572868
  112.5 0.8 copy-start.10
  119.8 7.1 %copy-start.6 = (f32[256,1024]{1,0:T(8,128)}, f32[256,1024]{1,0:T(8,128)S(1)}, u32[]{:S(2)}) copy-start(f32[256,1024]{1,0:T(8,128)S(1)} %get-tuple-element.5) | copy-start | bytes 3145732
  120.0 6.8 %collective-permute-start.4 = (bf16[1,4,16,1024]{3,2,1,0:T(8,128)(2,1)S(1)}, bf16[1,4,16,1024]{3,2,1,0:T(8,128)(2,1)S(1)}, u32[]{:S(2)}, u32[]{:S(2)}) collective-permute-start(bf16[1,4,16,1024]{3,2,1,0:T(8,128)(2,1)S(1)} %bitcast.122), channel_id=1, source_target_pairs={{0,8},{8,16},{16,24},{24,0},{1,9},{9,17},{17,25},{25,1},{2,10},{10... | collective-permute-start | bytes 393224 | tf_op jit(solution)/shard_map/ppermute | solution.py:17
  127.0 8.2 %collective-permute-start.5 = (bf16[4,3,16,1024]{3,2,1,0:T(8,128)(2,1)S(1)}, bf16[4,3,16,1024]{3,2,1,0:T(8,128)(2,1)S(1)}, u32[]{:S(2)}, u32[]{:S(2)}) collective-permute-start(bf16[4,3,16,1024]{3,2,1,0:T(8,128)(2,1)S(1)} %pad_maximum_fusion.6), channel_id=1, source_target_pairs={{0,1},{1,2},{2,3},{3,4},{4,5},{5,6},{6,7},{7,0},{8,9},{9,10},{10,1... | collective-permute-start | bytes 1179656 | tf_op jit(solution)/shard_map/ppermute | solution.py:17
  135.2 1.6 copy-start.24
  137.6 1.2 copy-start.13
  138.3 1.7 copy-start.18
  139.9 1.2 copy-start.19
  141.2 1.2 copy-start.20
  149.6 5.0 %copy-start.9 = (bf16[4,4,8,1024]{3,2,1,0:T(8,128)(2,1)S(1)}, bf16[4,4,8,1024]{3,2,1,0:T(8,128)(2,1)}, u32[]{:S(2)}) copy-start(bf16[4,4,8,1024]{3,2,1,0:T(8,128)(2,1)} %copy-done.8) | copy-start | bytes 786436
  160.8 5.4 %collective-permute-start.6 = (bf16[4,3,16,1024]{3,2,1,0:T(8,128)(2,1)S(1)}, bf16[4,3,16,1024]{3,2,1,0:T(8,128)(2,1)S(1)}, u32[]{:S(2)}, u32[]{:S(2)}) collective-permute-start(bf16[4,3,16,1024]{3,2,1,0:T(8,128)(2,1)S(1)} %slice.193), channel_id=1, source_target_pairs={{0,7},{1,0},{2,1},{3,2},{4,3},{5,4},{6,5},{7,6},{8,15},{9,8},{10,9... | collective-permute-start | bytes 1179656 | tf_op jit(solution)/shard_map/ppermute | solution.py:17
  166.3 2.1 copy-start.23
  166.6 5.0 %collective-permute-start.7 = (bf16[1,4,16,1024]{3,2,1,0:T(8,128)(2,1)S(1)}, bf16[1,4,16,1024]{3,2,1,0:T(8,128)(2,1)S(1)}, u32[]{:S(2)}, u32[]{:S(2)}) collective-permute-start(bf16[1,4,16,1024]{3,2,1,0:T(8,128)(2,1)S(1)} %fusion.44), channel_id=1, source_target_pairs={{0,24},{8,0},{16,8},{24,16},{1,25},{9,1},{17,9},{25,17},{2,26},{10... | collective-permute-start | bytes 393224 | tf_op jit(solution)/shard_map/ppermute | solution.py:17
  171.8 1.2 copy-start.7
  172.0 53.8 %copy-start.1 = (bf16[1024,1536]{1,0:T(8,128)(2,1)S(1)}, bf16[1024,1536]{1,0:T(8,128)(2,1)}, u32[]{:S(2)}) copy-start(bf16[1024,1536]{1,0:T(8,128)(2,1)} %param.14) | copy-start | bytes 9437188
  215.8 9.3 %all-to-all-start.2 = ((bf16[8,4,1024]{2,1,0:T(4,128)(2,1)}), bf16[8,4,1024]{2,1,0:T(4,128)(2,1)S(1)}, u32[]{:S(2)}, u32[]{:S(2)}) async-start(bf16[8,4,1024]{2,1,0:T(4,128)(2,1)} %multiply_convert_fusion.4), calls=%async_computation.2 | async-start | bytes 131072 | tf_op jit(solution)/shard_map/all_to_all | solution.py:204
where the time goes:
time: 227 us; the launch traced here: 226 us
  local copies, waits for them, and re-layouts  64.8 us (29%)
  blocking collectives  38.9 us (17%)
  waiting for transfers between devices  33.6 us (15%)
  matrix products  27.6 us (12%)
  other arithmetic  27.1 us (12%)
  starting transfers between devices  22.5 us (10%)
  between operations  11.3 us (5%)
    psum x1, blocking collectives, per_device(): mask_total = lax.psum(local_total, ('tm', 'row'))  38.9 us
    ppermute x8, waiting for transfers between devices, from_behind(): return lax.ppermute(value, axis, pairs)  26.6 us
    dot_general x2, matrix products, window_core(): jnp.dot(normed.reshape(-1, model_width), w_qkv, preferred_element_type=jn...  11 us
    reshape x2, local copies, waits for them, and re-layouts, window_core(): packed.reshape(frame_count // WT, WT, row_count // WH, WH, column_count /...  9.87 us
    unnamed x52, local copies, waits for them, and re-layouts  9.32 us
    ppermute x8, starting transfers between devices, from_behind(): return lax.ppermute(value, axis, pairs)  8.87 us
    reshape x1, local copies, waits for them, and re-layouts, window_core(): packed.transpose(6, 0, 2, 4, 7, 1, 3, 5, 8)  5.33 us
    all_to_all x1, starting transfers between devices, per_device(): lax.all_to_all(sent_index, 'row', split_axis=0, concat_axis=0, tiled=True)  5.17 us
  transfers between devices with their start and end apart: 11, of which 8 were waited for; matrix products, arithmetic and copies ran while one was open for 15% of the time, Pallas kernels for 0%

commit v1 on v0

v1 whole, which is shorter than its diff:
```python
import functools
import math

import jax
import jax.numpy as jnp
from jax import lax
from jax.experimental import pallas as pl
from jax.experimental.pallas import tpu as pltpu
from jax.sharding import PartitionSpec as P

HEADS = 16
WT = 2
WH = 4
WW = 8
EPS = 1e-05
TILE = 16
LANES = 128
MESH = pl.DeviceIdType.MESH
F32 = jnp.float32
BF16 = jnp.bfloat16


def sinusoid(coordinate, channel_count):
    half_count = channel_count // 2
    frequency = jnp.exp(-math.log(10000.0) * jnp.arange(half_count, dtype=F32) / half_count)
    angles = coordinate.astype(F32)[..., None] * frequency
    return jnp.concatenate([jnp.sin(angles), jnp.cos(angles)], axis=-1)


def nt_dot(a, b):
    return lax.dot_general(a, b, (((1,), (1,)), ((), ())), preferred_element_type=F32)


def tn_dot(a, b):
    return lax.dot_general(a, b, (((0,), (0,)), ((), ())), preferred_element_type=F32)


def nn_dot(a, b):
    return jnp.dot(a, b, preferred_element_type=F32)


def norm_parts(values):
    center = values - jnp.mean(values, axis=-1, keepdims=True)
    scale = lax.rsqrt(jnp.mean(center * center, axis=-1, keepdims=True) + EPS)
    return center * scale, scale


def norm_grad(cotangent, normed, scale):
    return scale * (
        cotangent
        - jnp.mean(cotangent, axis=-1, keepdims=True)
        - normed * jnp.mean(cotangent * normed, axis=-1, keepdims=True)
    )


def spread_kernel(slabs, bands, x_ref, out_ref, send_sem, recv_sem):
    i, d = lax.axis_index("tm"), lax.axis_index("row")
    after = lax.rem(i + 1, slabs)
    before = lax.rem(i + slabs - 1, slabs)
    barrier = pltpu.get_barrier_semaphore()
    for o in range(1, bands):
        pl.semaphore_signal(
            barrier, inc=1, device_id=(i, lax.rem(d + o, bands)), device_id_type=MESH
        )
    for o in range(bands):
        pl.semaphore_signal(
            barrier, inc=1, device_id=(before, lax.rem(d + o, bands)), device_id_type=MESH
        )
    pl.semaphore_wait(barrier, 2 * bands - 1)
    copies = []
    for q, slab in ((1, after), (0, i)):
        for o in range(1 - q, bands):
            e = lax.rem(d + o, bands)
            copy = pltpu.make_async_remote_copy(
                src_ref=x_ref.at[e],
                dst_ref=out_ref.at[q * bands + d],
                send_sem=send_sem.at[q * bands + o],
                recv_sem=recv_sem.at[q * bands + o],
                device_id=(slab, e),
                device_id_type=MESH,
            )
            copy.start()
            copies.append((q, o, copy))
    out_ref[d] = x_ref[d]
    for q, o, copy in copies:
        s = lax.rem(d + bands - o, bands)
        arriving = pltpu.make_async_remote_copy(
            src_ref=x_ref.at[0],
            dst_ref=out_ref.at[q * bands + s],
            send_sem=send_sem.at[q * bands + o],
            recv_sem=recv_sem.at[q * bands + o],
            device_id=(i, lax.rem(d + 1, bands)),
            device_id_type=MESH,
        )
        arriving.wait_recv()
        copy.wait_send()


def collect_kernel(
    slabs, bands, x_ref, sum_ref, out_ref, total_ref,
    got, row_sums, slab_sums, mine,
    send_sem, recv_sem, row_send, row_recv, slab_send, slab_recv,
):
    i, d = lax.axis_index("tm"), lax.axis_index("row")
    after = lax.rem(i + 1, slabs)
    before = lax.rem(i + slabs - 1, slabs)
    barrier = pltpu.get_barrier_semaphore()
    for o in range(1, bands):
        pl.semaphore_signal(
            barrier, inc=1, device_id=(i, lax.rem(d + o, bands)), device_id_type=MESH
        )
    for o in range(bands):
        pl.semaphore_signal(
            barrier, inc=1, device_id=(after, lax.rem(d + o, bands)), device_id_type=MESH
        )
    for o in range(1, slabs):
        pl.semaphore_signal(
            barrier, inc=1, device_id=(lax.rem(i + o, slabs), d), device_id_type=MESH
        )
    pl.semaphore_wait(barrier, 2 * bands - 1 + slabs - 1)

    sums = []
    for o in range(1, bands):
        copy = pltpu.make_async_remote_copy(
            src_ref=sum_ref,
            dst_ref=row_sums.at[d],
            send_sem=row_send.at[o],
            recv_sem=row_recv.at[o],
            device_id=(i, lax.rem(d + o, bands)),
            device_id_type=MESH,
        )
        copy.start()
        sums.append(copy)
    copies = []
    for q, slab in ((1, before), (0, i)):
        for o in range(1 - q, bands):
            s = lax.rem(d + o, bands)
            copy = pltpu.make_async_remote_copy(
                src_ref=x_ref.at[q * bands + s],
                dst_ref=got.at[q * bands + d],
                send_sem=send_sem.at[q * bands + o],
                recv_sem=recv_sem.at[q * bands + o],
                device_id=(slab, s),
                device_id_type=MESH,
            )
            copy.start()
            copies.append((q, o, copy))
    got[d] = x_ref[d]
    row_sums[d] = sum_ref[...]
    for o, copy in enumerate(sums, 1):
        s = lax.rem(d + bands - o, bands)
        pltpu.make_async_remote_copy(
            src_ref=sum_ref,
            dst_ref=row_sums.at[s],
            send_sem=row_send.at[o],
            recv_sem=row_recv.at[o],
            device_id=(i, lax.rem(d + 1, bands)),
            device_id_type=MESH,
        ).wait_recv()
        copy.wait_send()
    total = row_sums[0]
    for s in range(1, bands):
        total = total + row_sums[s]
    mine[...] = total
    slab_sums[i] = total
    sums = []
    for o in range(1, slabs):
        copy = pltpu.make_async_remote_copy(
            src_ref=mine,
            dst_ref=slab_sums.at[i],
            send_sem=slab_send.at[o],
            recv_sem=slab_recv.at[o],
            device_id=(lax.rem(i + o, slabs), d),
            device_id_type=MESH,
        )
        copy.start()
        sums.append(copy)
    for q, o, copy in copies:
        s = lax.rem(d + bands - o, bands)
        pltpu.make_async_remote_copy(
            src_ref=x_ref.at[0],
            dst_ref=got.at[q * bands + s],
            send_sem=send_sem.at[q * bands + o],
            recv_sem=recv_sem.at[q * bands + o],
            device_id=(i, lax.rem(d + 1, bands)),
            device_id_type=MESH,
        ).wait_recv()
        copy.wait_send()
    for e in range(bands):
        f = (e + 1) % bands
        value = got[e, 1].astype(F32) + got[f, 0].astype(F32)
        value = value + got[bands + e, 1].astype(F32) + got[bands + f, 0].astype(F32)
        out_ref[e] = value.astype(BF16)
    for o, copy in enumerate(sums, 1):
        s = lax.rem(i + slabs - o, slabs)
        pltpu.make_async_remote_copy(
            src_ref=mine,
            dst_ref=slab_sums.at[s],
            send_sem=slab_send.at[o],
            recv_sem=slab_recv.at[o],
            device_id=(lax.rem(i + 1, slabs), d),
            device_id_type=MESH,
        ).wait_recv()
        copy.wait_send()
    total = slab_sums[0]
    for s in range(1, slabs):
        total = total + slab_sums[s]
    total_ref[...] = total


def block_kernel(
    slots, grid,
    shift_ref, recv_ref, token_ref, mask_ref, pos_t_ref, pos_h_ref, pos_c_ref,
    w_qkv_ref, w_out_ref, w_head_ref, own_ref, rows_ref, frames_ref, corner_ref,
    picked_ref, sum_ref,
    joined, pix, probs, mixed, d_qkv,
):
    frames, rows, columns = grid
    groups = columns // WW
    tokens = frames * rows * columns
    width = mask_ref.shape[1]
    head_dim = width // HEADS
    parts = TILE // slots
    chunk = width // parts
    total_rows = recv_ref.shape[0]
    rim_t, rim_h = WT - 1, WH - 1

    index = recv_ref[:, chunk:].astype(F32)
    index = jnp.concatenate([index] * (tokens // LANES), axis=1)
    pieces = []
    for block in range(total_rows // TILE):
        q = block // (total_rows // TILE // 2)
        line = token_ref[2 * q + block % 2 : 2 * q + block % 2 + 1, :]
        pieces.append(jnp.broadcast_to(line, (TILE, tokens)))
    hit = (index == jnp.concatenate(pieces, axis=0)).astype(F32)
    part_of = lax.broadcasted_iota(jnp.int32, (total_rows, tokens), 0) // slots % parts
    part_of_t = lax.broadcasted_iota(jnp.int32, (tokens, total_rows), 1) // slots % parts
    hit_t = hit.T
    seen = jnp.max(hit_t, axis=1, keepdims=True)
    masked = 1.0 - seen
    packed_rows = recv_ref[:, :chunk]
    start = jnp.concatenate(
        [
            nn_dot(jnp.where(part_of_t == j, hit_t, 0.0).astype(BF16), packed_rows)
            for j in range(parts)
        ],
        axis=1,
    )
    start = jnp.where(seen > 0, start, mask_ref[...].astype(F32))

    order = [
        (fw, hw, g, ft, r)
        for fw in range(frames // WT)
        for hw in range(rows // WH)
        for g in range(groups)
        for ft in range(WT)
        for r in range(WH)
    ]
    pieces = []
    for fw, hw, g, ft, r in order:
        t_line = g * frames + fw * WT + ft
        h_line = g * rows + hw * WH + r
        pieces.append(
            jnp.concatenate(
                [
                    jnp.broadcast_to(pos_t_ref[t_line : t_line + 1], (WW, pos_t_ref.shape[1])),
                    jnp.broadcast_to(pos_h_ref[h_line : h_line + 1], (WW, pos_h_ref.shape[1])),
                    pos_c_ref[g * WW : (g + 1) * WW],
                ],
                axis=1,
            )
        )
    embedded = (start + jnp.concatenate(pieces, axis=0)).astype(BF16).astype(F32)

    normed, scale = norm_parts(embedded)
    qkv = nn_dot(normed.astype(BF16), w_qkv_ref[...]).astype(BF16)

    window = WT * WH * WW
    span = 2 * window
    pair = 2 * head_dim
    same = (
        lax.broadcasted_iota(jnp.int32, (span, span), 0) // window
        == lax.broadcasted_iota(jnp.int32, (span, span), 1) // window
    )
    lane = lax.broadcasted_iota(jnp.int32, (span, pair), 1) // head_dim
    zero = jnp.zeros((span, pair), BF16)

    def block_of(values, b, at):
        return values[b * span : (b + 1) * span, at : at + pair]

    for b in range(tokens // span):
        for p in range(HEADS // 2):
            q = block_of(qkv, b, p * pair)
            k = block_of(qkv, b, width + p * pair)
            v = block_of(qkv, b, 2 * width + p * pair)
            out = None
            for h in range(2):
                scores = nt_dot(q, jnp.where(lane == h, k, zero)) * head_dim ** (-0.5)
                scores = jnp.where(same, scores, -jnp.inf)
                weights = jnp.exp(scores - jnp.max(scores, axis=-1, keepdims=True))
                weights = weights / jnp.sum(weights, axis=-1, keepdims=True)
                probs[(b * HEADS // 2 + p) * 2 + h] = weights
                part = nn_dot(weights.astype(BF16), jnp.where(lane == h, v, zero))
                out = part if out is None else out + part
            mixed[b * span : (b + 1) * span, p * pair : (p + 1) * pair] = out.astype(BF16)
    attn = nn_dot(mixed[...], w_out_ref[...]).astype(BF16)
    residual = embedded + attn.astype(F32)

    for t in range(frames):
        for h in range(rows):
            joined[(t + rim_t) * (rows + rim_h) + h + rim_h] = own_ref[t, h]
        for h in range(rim_h):
            joined[(t + rim_t) * (rows + rim_h) + h] = rows_ref[t, h]
    for t in range(rim_t):
        for h in range(rows):
            joined[t * (rows + rim_h) + h + rim_h] = frames_ref[t, h]
        for h in range(rim_h):
            joined[t * (rows + rim_h) + h] = corner_ref[t, h]
    for n, (fw, hw, g, ft, r) in enumerate(order):
        t = fw * WT + ft + rim_t - shift_ref[0, g]
        h = hw * WH + r + rim_h - shift_ref[1, g]
        pix[n * WW : (n + 1) * WW, :] = joined[t * (rows + rim_h) + h][
            g * WW : (g + 1) * WW, :
        ].astype(F32)
    group_size = pix.shape[1] // 3
    targets = []
    for c in range(3):
        raw = pix[:, c * group_size : (c + 1) * group_size]
        center = raw - jnp.mean(raw, axis=-1, keepdims=True)
        spread = jnp.sqrt(jnp.sum(center * center, axis=-1, keepdims=True) / (group_size - 1))
        targets.append(center / (spread + 1e-06))
    target = jnp.concatenate(targets, axis=1)

    normed_out, scale_out = norm_parts(residual)
    predicted = nn_dot(normed_out.astype(BF16), w_head_ref[...])
    errors = (predicted - target) * masked
    d_normed_out = nt_dot(errors.astype(BF16), w_head_ref[...]).astype(BF16).astype(F32)
    grad_residual = norm_grad(d_normed_out, normed_out, scale_out)
    d_mixed = nt_dot(grad_residual.astype(BF16), w_out_ref[...]).astype(BF16)

    for b in range(tokens // span):
        for p in range(HEADS // 2):
            q = block_of(qkv, b, p * pair)
            k = block_of(qkv, b, width + p * pair)
            v = block_of(qkv, b, 2 * width + p * pair)
            d_out = block_of(d_mixed, b, p * pair)
            dq = dk = dv = None
            for h in range(2):
                mine = lane == h
                weights = probs[(b * HEADS // 2 + p) * 2 + h]
                d_weights = nt_dot(d_out, jnp.where(mine, v, zero)).astype(BF16).astype(F32)
                inner = jnp.sum(weights * d_weights, axis=-1, keepdims=True)
                d_scores = weights * (d_weights - inner) * head_dim ** (-0.5)
                d_scores = d_scores.astype(BF16)
                terms = (
                    nn_dot(d_scores, jnp.where(mine, k, zero)),
                    tn_dot(d_scores, jnp.where(mine, q, zero)),
                    tn_dot(weights.astype(BF16), jnp.where(mine, d_out, zero)),
                )
                if h == 0:
                    dq, dk, dv = terms
                else:
                    dq, dk, dv = dq + terms[0], dk + terms[1], dv + terms[2]
            for m, value in enumerate((dq, dk, dv)):
                at = m * width + p * pair
                d_qkv[b * span : (b + 1) * span, at : at + pair] = value.astype(BF16)
    d_normed = nt_dot(d_qkv[...], w_qkv_ref[...]).astype(BF16).astype(F32)
    grad = grad_residual + norm_grad(d_normed, normed, scale)

    line = jnp.sum(grad * masked, axis=0, keepdims=True)
    for j in range(width // LANES):
        sum_ref[j : j + 1, :] = line[:, j * LANES : (j + 1) * LANES]
    rounded = grad.astype(BF16)
    picked = None
    for j in range(parts):
        term = nn_dot(
            jnp.where(part_of == j, hit, 0.0).astype(BF16), rounded[:, j * chunk : (j + 1) * chunk]
        )
        picked = term if picked is None else picked + term
    picked_ref[...] = picked.astype(BF16)


def per_device(visible, slot_pos, window_shift, mask_token, w_qkv, w_out, w_head, pixels):
    frames, rows, columns, pixel_count = pixels.shape
    width = mask_token.shape[0]
    tokens = frames * rows * columns
    bands, slots = slot_pos.shape[2:]
    slabs = lax.axis_size("tm")
    groups = columns // WW
    parts = TILE // slots
    chunk = width // parts
    rim_t, rim_h = WT - 1, WH - 1
    i, d = lax.axis_index("tm"), lax.axis_index("row")
    vmem = pl.BlockSpec(memory_space=pltpu.VMEM)

    both = ("tm", "row")
    slab_ring = [(a, (a + 1) % slabs) for a in range(slabs)]
    band_ring = [(a, (a + 1) % bands) for a in range(bands)]
    corner_ring = [
        (a * bands + b, (a + 1) % slabs * bands + (b + 1) % bands)
        for a in range(slabs)
        for b in range(bands)
    ]
    row_halo = lax.ppermute(pixels[:, rows - rim_h :], "row", band_ring)
    frame_halo = lax.ppermute(pixels[frames - rim_t :], "tm", slab_ring)
    corner_halo = lax.ppermute(pixels[frames - rim_t :, rows - rim_h :], both, corner_ring)

    packed = visible.reshape(bands, slots, parts, chunk).transpose(0, 2, 1, 3)
    packed = packed.reshape(bands, TILE, chunk)
    index = jnp.broadcast_to(
        slot_pos.reshape(bands, 1, slots, 1), (bands, parts, slots, LANES)
    ).reshape(bands, TILE, LANES)
    packed = jnp.concatenate([packed, index.astype(BF16)], axis=-1)
    packed = jnp.stack([jnp.roll(packed, 1, axis=0), packed], axis=1)
    wide = chunk + LANES
    received = pl.pallas_call(
        functools.partial(spread_kernel, slabs, bands),
        out_shape=jax.ShapeDtypeStruct((2 * bands, 2, TILE, wide), BF16),
        in_specs=[vmem],
        out_specs=vmem,
        scratch_shapes=[
            pltpu.SemaphoreType.DMA((2 * bands,)),
            pltpu.SemaphoreType.DMA((2 * bands,)),
        ],
        compiler_params=pltpu.CompilerParams(collective_id=0, has_side_effects=True),
        name="spread",
    )(packed)

    n = jnp.arange(tokens, dtype=jnp.int32)
    column = n % WW
    r = n // WW % WH
    ft = n // (WW * WH) % WT
    g = n // (WW * WH * WT) % groups
    hw = n // (WW * WH * WT * groups) % (rows // WH)
    fw = n // (WW * WH * WT * groups * (rows // WH))
    t_shift = sum(jnp.where(g == a, window_shift[0, a], 0) for a in range(groups))
    h_shift = sum(jnp.where(g == a, window_shift[1, a], 0) for a in range(groups))
    t = fw * WT + ft - t_shift
    h = hw * WH + r - h_shift
    local = (t % frames * rows + h % rows) * columns + g * WW + column
    token_index = jnp.stack(
        [
            jnp.where(((t < 0) == (q == 1)) & ((h < 0) == (k == 0)), local, -2)
            for q in range(2)
            for k in range(2)
        ]
    ).astype(F32)
    quarter = width // 4
    rest = (width - quarter) // 2
    t_all = (i * frames + jnp.arange(frames) - window_shift[0][:, None]) % (frames * slabs)
    h_all = (d * rows + jnp.arange(rows) - window_shift[1][:, None]) % (rows * bands)
    pos_t = sinusoid(t_all.reshape(-1), quarter)
    pos_h = sinusoid(h_all.reshape(-1), rest)
    pos_c = sinusoid(jnp.arange(columns), width - quarter - rest)

    total_rows = 2 * bands * 2 * TILE
    flops = 4 * tokens * width * (w_qkv.shape[1] + width + pixel_count)
    picked, partial_sum = pl.pallas_call(
        functools.partial(block_kernel, slots, (frames, rows, columns)),
        out_shape=(
            jax.ShapeDtypeStruct((total_rows, chunk), BF16),
            jax.ShapeDtypeStruct((width // LANES, LANES), F32),
        ),
        in_specs=[pl.BlockSpec(memory_space=pltpu.SMEM)] + [vmem] * 13,
        out_specs=(vmem, vmem),
        scratch_shapes=[
            pltpu.VMEM(((frames + rim_t) * (rows + rim_h), columns, pixel_count), BF16),
            pltpu.VMEM((tokens, pixel_count), F32),
            pltpu.VMEM(
                (HEADS * tokens // (2 * WT * WH * WW), 2 * WT * WH * WW, 2 * WT * WH * WW), F32
            ),
            pltpu.VMEM((tokens, width), BF16),
            pltpu.VMEM((tokens, 3 * width), BF16),
        ],
        compiler_params=pltpu.CompilerParams(vmem_limit_bytes=56 * 2**20),
        cost_estimate=pl.CostEstimate(
            flops=flops, bytes_accessed=16 * 2**20, transcendentals=HEADS * tokens * 128
        ),
        name="block",
    )(
        window_shift, received.reshape(total_rows, wide), token_index, mask_token[None, :],
        pos_t, pos_h, pos_c, w_qkv, w_out, w_head, pixels, row_halo, frame_halo, corner_halo,
    )

    lines = width // LANES
    returned, total = pl.pallas_call(
        functools.partial(collect_kernel, slabs, bands),
        out_shape=(
            jax.ShapeDtypeStruct((bands, TILE, chunk), BF16),
            jax.ShapeDtypeStruct((lines, LANES), F32),
        ),
        in_specs=[vmem, vmem],
        out_specs=(vmem, vmem),
        scratch_shapes=[
            pltpu.VMEM((2 * bands, 2, TILE, chunk), BF16),
            pltpu.VMEM((bands, lines, LANES), F32),
            pltpu.VMEM((slabs, lines, LANES), F32),
            pltpu.VMEM((lines, LANES), F32),
            pltpu.SemaphoreType.DMA((2 * bands,)),
            pltpu.SemaphoreType.DMA((2 * bands,)),
            pltpu.SemaphoreType.DMA((bands,)),
            pltpu.SemaphoreType.DMA((bands,)),
            pltpu.SemaphoreType.DMA((slabs,)),
            pltpu.SemaphoreType.DMA((slabs,)),
        ],
        compiler_params=pltpu.CompilerParams(collective_id=1, has_side_effects=True),
        name="collect",
    )(picked.reshape(2 * bands, 2, TILE, chunk), partial_sum)
    d_visible = returned.reshape(bands, parts, slots, chunk).transpose(0, 2, 1, 3)
    grad_scale = (tokens * slabs * bands) ** (-0.5)
    return d_visible.reshape(visible.shape), total.reshape(width) * grad_scale


def solution(mesh):
    placed = (
        P("tm", "row", None, None, None),
        P("tm", "row", None, None),
        P(),
        P(),
        P(),
        P(),
        P(),
        P("tm", "row", None, None),
    )
    return jax.shard_map(
        per_device,
        mesh=mesh,
        in_specs=placed,
        out_specs=(P("tm", "row", None, None, None), P()),
        check_vma=False,
    )
```

time: 227 us -> 76 us (0.33)
  local copies, waits for them, and re-layouts: 64.8 us -> 9.33 us
  Pallas kernels: 0 us -> 48.8 us
  blocking collectives: 38.9 us -> 0 us
  waiting for transfers between devices: 33.6 us -> 0.01 us
  matrix products: 27.6 us -> 0 us
  starting transfers between devices: 22.5 us -> 5.69 us
  other arithmetic: 27.1 us -> 10.9 us
  between operations: 11.3 us -> 0.79 us
    pallas_call x0 -> x3, Pallas kernels: none -> 48.8 us  [the longest x1 25.2 us: per_device(): pl.pallas_call(functools.partial(block_kernel, slots, (frames, rows, colu...]
    psum x1 -> x0, blocking collectives: 38.9 us -> none  [per_device(): mask_total = lax.psum(local_total, ('tm', 'row'))]
    ppermute x8 -> x3, waiting for transfers between devices: 26.6 us -> 0.01 us  [the longest x1 0.01 us: per_device(): lax.ppermute(pixels[frames - rim_t:, rows - rim_h:], both, corner_ring)]
    dot_general x10 -> x0, matrix products: 23.9 us -> none  [the longest x2 11 us: window_core(): jnp.dot(normed.reshape(-1, model_width), w_qkv, preferred_element_type=jn...]
    all_to_all x3 -> x0, starting transfers between devices: 13.6 us -> none  [the longest x1 5.17 us: per_device(): lax.all_to_all(sent_index, 'row', split_axis=0, concat_axis=0, tiled=True)]
    reshape x5 -> x2, local copies, waits for them, and re-layouts: 15.9 us -> 2.35 us  [the longest x1 1.49 us: per_device(): returned.reshape(bands, parts, slots, chunk).transpose(0, 2, 1, 3)]
    reduce_sum x9 -> x0, other arithmetic: 8.77 us -> none  [the longest x4 2.58 us: layer_norm(): center = values - jnp.mean(values, axis=-1, keepdims=True)]
    unnamed x52 -> x8, local copies, waits for them, and re-layouts: 9.32 us -> 0.9 us
  transfers between devices with their start and end apart: 11 -> 3, of which waited for: 8 -> 0; matrix products, arithmetic and copies ran while one was open for 15% -> 20% of each run, Pallas kernels for 0% -> 17%
where the time goes in v1:
time: 76 us; the launch traced here: 75.5 us
  Pallas kernels  48.8 us (64%)
  other arithmetic  10.9 us (14%)
  local copies, waits for them, and re-layouts  9.33 us (12%)
  starting transfers between devices  5.69 us (7%)
  between operations  0.79 us (1%)
    pallas_call x1, Pallas kernels, per_device(): pl.pallas_call(functools.partial(block_kernel, slots, (frames, rows, colu...  25.2 us
    pallas_call x1, Pallas kernels, per_device(): pl.pallas_call(functools.partial(spread_kernel, slabs, bands), out_shape=...  12.6 us
    pallas_call x1, Pallas kernels, per_device(): pl.pallas_call(functools.partial(collect_kernel, slabs, bands), out_shape...  11 us
    select_n x2, other arithmetic, per_device(): jnp.where(((t < 0) == (q == 1)) & ((h < 0) == (k == 0)), local, -2)  5.11 us
    ppermute x1, starting transfers between devices, per_device(): frame_halo = lax.ppermute(pixels[frames - rim_t:], 'tm', slab_ring)  2.64 us
    ppermute x1, starting transfers between devices, per_device(): lax.ppermute(pixels[frames - rim_t:, rows - rim_h:], both, corner_ring)  2.54 us
    concatenate x3, other arithmetic, sinusoid(): return jnp.concatenate([jnp.sin(angles), jnp.cos(angles)], axis=-1)  1.95 us
  transfers between devices with their start and end apart: 3, of which 0 were waited for; matrix products, arithmetic and copies ran while one was open for 20% of the time, Pallas kernels for 17%

profile of v1, /device:TPU:0, one launch (start us, length us, event | category | flops | bytes accessed | tf_op | source)
XLA Modules:
  0.0 75.5 jit_solution(17899196771431443204)
XLA Ops:
  0.6 0.0 copy-start
  0.6 1.1 %slice.43 = bf16[4,3,16,1536]{3,2,1,0:T(8,128)(2,1)S(1)} slice(bf16[4,4,16,1536]{3,2,1,0:T(8,128)(2,1)} %own_ref.1), slice={[0:4], [1:4], [0:16], [0:1536]} | slice | bytes 1179648 | tf_op jit(solution)/shard_map/slice | solution.py:404
  1.8 0.5 collective-permute-start
  2.3 0.9 %slice.44 = bf16[1,4,16,1536]{3,2,1,0:T(8,128)(2,1)S(1)} slice(bf16[4,4,16,1536]{3,2,1,0:T(8,128)(2,1)} %own_ref.1), slice={[3:4], [0:4], [0:16], [0:1536]} | slice | bytes 393216 | tf_op jit(solution)/shard_map/slice | solution.py:405
  3.2 2.6 %collective-permute-start.1 = (bf16[1,4,16,1536]{3,2,1,0:T(8,128)(2,1)S(1)}, bf16[1,4,16,1536]{3,2,1,0:T(8,128)(2,1)S(1)}, u32[]{:S(2)}, u32[]{:S(2)}) collective-permute-start(bf16[1,4,16,1536]{3,2,1,0:T(8,128)(2,1)S(1)} %slice.44), channel_id=1, source_target_pairs={{0,8},{8,16},{16,24},{24,0},{1,9},{9,17},{17,25},{25,1},{2,10},{10... | collective-permute-start | bytes 589832 | tf_op jit(solution)/shard_map/ppermute | solution.py:405
  5.8 0.9 %slice.45 = bf16[1,3,16,1536]{3,2,1,0:T(8,128)(2,1)S(1)} slice(bf16[4,4,16,1536]{3,2,1,0:T(8,128)(2,1)} %own_ref.1), slice={[3:4], [1:4], [0:16], [0:1536]} | slice | bytes 294912 | tf_op jit(solution)/shard_map/slice | solution.py:406
  6.8 2.5 %collective-permute-start.2 = (bf16[1,3,16,1536]{3,2,1,0:T(8,128)(2,1)S(1)}, bf16[1,3,16,1536]{3,2,1,0:T(8,128)(2,1)S(1)}, u32[]{:S(2)}, u32[]{:S(2)}) collective-permute-start(bf16[1,3,16,1536]{3,2,1,0:T(8,128)(2,1)S(1)} %slice.45), channel_id=1, source_target_pairs={{0,9},{1,10},{2,11},{3,12},{4,13},{5,14},{6,15},{7,8},{8,17},{9,18... | collective-permute-start | bytes 442376 | tf_op jit(solution)/shard_map/ppermute | solution.py:406
  9.3 1.4 %fusion.22 = (s32[1,1]{1,0:T(1,128)}, s32[1,1]{1,0:T(1,128)}, s32[1,1]{1,0:T(1,128)}, s32[1,1]{1,0:T(1,128)}) fusion(s32[2,2]{1,0:T(2,128)} %shift_ref.1), kind=kLoop, calls=%fused_computation.95 | loop fusion | bytes 32 | tf_op jit(solution)/shard_map/slice | solution.py:437
  10.7 2.6 %and_select_fusion = (s32[1,256]{1,0:T(1,128)S(1)}, s32[1,256]{1,0:T(1,128)S(1)}) fusion(s32[]{:T(128)} %bitcast.9, s32[]{:T(128)} %bitcast.8, s32[]{:T(128)} %bitcast.11, s32[]{:T(128)} %bitcast.10), kind=kLoop, calls=%fused_computation.27 | loop fusion | flops 27648 | bytes 2064 | tf_op jit(solution)/shard_map/jit(_where)/select_n | solution.py:443
  13.3 2.6 %and_select_fusion.2 = (s32[1,256]{1,0:T(1,128)S(1)}, s32[1,256]{1,0:T(1,128)S(1)}) fusion(s32[]{:T(128)} %bitcast.9, s32[]{:T(128)} %bitcast.8, s32[]{:T(128)} %bitcast.11, s32[]{:T(128)} %bitcast.10), kind=kLoop, calls=%fused_computation.29 | loop fusion | flops 27904 | bytes 2064 | tf_op jit(solution)/shard_map/jit(_where)/select_n | solution.py:443
  15.9 0.9 %reshape.482 = bf16[8,16,256]{2,1,0:T(8,128)(2,1)S(1)} reshape(bf16[8,4,4,256]{3,2,1,0:T(4,128)(2,1)} %bitcast.29) | data formatting | bytes 131072 | tf_op jit(solution)/shard_map/reshape | solution.py:409
  16.7 0.7 convert_bitcast_fusion
  17.4 0.1 copy.11
  17.5 0.1 broadcast_in_dim.44
  17.6 0.8 %slice_bitcast_fusion = (s32[2]{0:T(128)S(1)}, s32[2]{0:T(128)S(1)}) fusion(s32[2,2]{1,0:T(2,128)} %shift_ref.1), kind=kLoop, calls=%fused_computation.86 | loop fusion | bytes 32 | tf_op jit(solution)/shard_map/sub | solution.py:451
  18.4 0.1 broadcast_subtract_fusion
  18.5 0.1 sub.133
  18.6 0.1 sub.128
  18.7 0.1 multiply_sine_fusion.1
  18.8 0.7 pad_maximum_fusion.3.pos_h_ref
  19.5 0.1 multiply_sine_fusion.2
  19.6 0.6 pad_maximum_fusion.4.pos_t_ref
  20.2 0.7 pad_maximum_fusion.x_ref
  20.9 0.1 multiply_sine_fusion
  21.1 0.6 add_convert_fusion.token_ref
  21.7 12.6 %spread.1 = bf16[16,2,16,384]{3,2,1,0:T(8,128)(2,1)} custom-call(bf16[8,2,16,384]{3,2,1,0:T(8,128)(2,1)} %pad_maximum_fusion.x_ref), custom_call_target="tpu_custom_call" | custom-call | tf_op jit(solution)/shard_map/spread/pallas_call | solution.py:416
  34.3 0.0 copy-done
  34.3 0.6 broadcast_in_dim.50.mask_ref
  34.9 0.7 pad_maximum_fusion.2.pos_c_ref
  35.6 0.0 collective-permute-done.2.corner_ref
  35.6 0.0 copy-start.3
  35.6 0.0 collective-permute-done.1.frames_ref
  35.6 0.0 copy-start.2
  35.6 0.0 collective-permute-done.rows_ref
  35.6 0.0 copy-start.1
  35.6 0.6 copy-done.3
  36.2 0.1 copy-done.2
  36.3 0.2 copy-done.1
  36.5 25.2 %block.1 = (bf16[512,256]{1,0:T(8,128)(2,1)}, f32[8,128]{1,0:T(8,128)}) custom-call(s32[2,2]{1,0:T(2,128)} %shift_ref.1, bf16[512,384]{1,0:T(8,128)(2,1)} %bitcast.27, f32[4,256]{1,0:T(4,128)} %add_convert_fusion.token_ref, bf16[1,1024]{1,0:T(2,128)(2,1)} %broadcast_in_dim.50.mask_ref, f32[8,256]{1,0:T(8,128)} %pad_maximum_fusion.4.pos_t_ref, ...), custom_call_target="tpu_custom_call" | custom-call | flops 5905580032 | bytes 16777216 | tf_op jit(solution)/shard_map/block/pallas_call | solution.py:458
  61.7 11.0 %collect.1 = (bf16[8,16,256]{2,1,0:T(8,128)(2,1)}, f32[8,128]{1,0:T(8,128)}) custom-call(bf16[16,2,16,256]{3,2,1,0:T(8,128)(2,1)} %bitcast.28, f32[8,128]{1,0:T(8,128)} %get-tuple-element.7.sum_ref), custom_call_target="tpu_custom_call" | custom-call | tf_op jit(solution)/shard_map/collect/pallas_call | solution.py:486
  72.7 1.5 %reshape.485 = bf16[8,4,4,256]{3,2,1,0:T(4,128)(2,1)} reshape(bf16[8,16,256]{2,1,0:T(8,128)(2,1)} %get-tuple-element.8) | data formatting | bytes 131072 | tf_op jit(solution)/shard_map/reshape | solution.py:509
  74.2 1.3 %multiply_bitcast_fusion = f32[1024]{0:T(1024)} fusion(f32[8,128]{1,0:T(8,128)} %get-tuple-element.9), kind=kLoop, calls=%fused_computation.26 | loop fusion | flops 1024 | bytes 8192 | tf_op jit(solution)/shard_map/mul | solution.py:511
  (11 shorter events, 0.1 us)
Async XLA Ops:
  0.6 33.7 %copy-start = (bf16[1024]{0:T(1024)(128)(2,1)S(1)}, bf16[1024]{0:T(1024)(128)(2,1)}, u32[]{:S(2)}) copy-start(bf16[1024]{0:T(1024)(128)(2,1)} %param.11) | copy-start | bytes 6148
  1.8 33.9 %collective-permute-start = (bf16[4,3,16,1536]{3,2,1,0:T(8,128)(2,1)S(1)}, bf16[4,3,16,1536]{3,2,1,0:T(8,128)(2,1)S(1)}, u32[]{:S(2)}, u32[]{:S(2)}) collective-permute-start(bf16[4,3,16,1536]{3,2,1,0:T(8,128)(2,1)S(1)} %slice.43), channel_id=1, source_target_pairs={{0,1},{1,2},{2,3},{3,4},{4,5},{5,6},{6,7},{7,0},{8,9},{9,10},{10,1... | collective-permute-start | bytes 1769480 | tf_op jit(solution)/shard_map/ppermute | solution.py:404
  3.2 32.4 %collective-permute-start.1 = (bf16[1,4,16,1536]{3,2,1,0:T(8,128)(2,1)S(1)}, bf16[1,4,16,1536]{3,2,1,0:T(8,128)(2,1)S(1)}, u32[]{:S(2)}, u32[]{:S(2)}) collective-permute-start(bf16[1,4,16,1536]{3,2,1,0:T(8,128)(2,1)S(1)} %slice.44), channel_id=1, source_target_pairs={{0,8},{8,16},{16,24},{24,0},{1,9},{9,17},{17,25},{25,1},{2,10},{10... | collective-permute-start | bytes 589832 | tf_op jit(solution)/shard_map/ppermute | solution.py:405
  6.8 28.8 %collective-permute-start.2 = (bf16[1,3,16,1536]{3,2,1,0:T(8,128)(2,1)S(1)}, bf16[1,3,16,1536]{3,2,1,0:T(8,128)(2,1)S(1)}, u32[]{:S(2)}, u32[]{:S(2)}) collective-permute-start(bf16[1,3,16,1536]{3,2,1,0:T(8,128)(2,1)S(1)} %slice.45), channel_id=1, source_target_pairs={{0,9},{1,10},{2,11},{3,12},{4,13},{5,14},{6,15},{7,8},{8,17},{9,18... | collective-permute-start | bytes 442376 | tf_op jit(solution)/shard_map/ppermute | solution.py:406
  35.6 0.7 copy-start.3
  35.6 0.7 copy-start.2
  35.6 0.9 %copy-start.1 = (bf16[4,3,16,1536]{3,2,1,0:T(8,128)(2,1)}, bf16[4,3,16,1536]{3,2,1,0:T(8,128)(2,1)S(1)}, u32[]{:S(2)}) copy-start(bf16[4,3,16,1536]{3,2,1,0:T(8,128)(2,1)S(1)} %collective-permute-done.rows_ref) | copy-start | bytes 1769476

commit v2 on v1

--- a/solution.py
+++ b/solution.py
@@ -20,11 +20,13 @@
 BF16 = jnp.bfloat16
 
 
-def sinusoid(coordinate, channel_count):
+def sinusoid(coordinates, channel_count):
     half_count = channel_count // 2
-    frequency = jnp.exp(-math.log(10000.0) * jnp.arange(half_count, dtype=F32) / half_count)
-    angles = coordinate.astype(F32)[..., None] * frequency
-    return jnp.concatenate([jnp.sin(angles), jnp.cos(angles)], axis=-1)
+    lane = lax.broadcasted_iota(jnp.int32, (1, channel_count), 1)
+    late = lane >= half_count
+    step = jnp.where(late, lane - half_count, lane).astype(F32)
+    angles = coordinates * jnp.exp(-math.log(10000.0) * step / half_count)
+    return jnp.where(late, jnp.cos(angles), jnp.sin(angles))
 
 
 def nt_dot(a, b):
@@ -53,7 +55,11 @@
     )
 
 
-def spread_kernel(slabs, bands, x_ref, out_ref, send_sem, recv_sem):
+def spread_kernel(
+    slabs, bands, slot_ref, visible_ref, pixel_ref,
+    out_ref, row_ref, frame_ref, corner_ref,
+    x_ref, send_sem, recv_sem, halo_send, halo_recv,
+):
     i, d = lax.axis_index("tm"), lax.axis_index("row")
     after = lax.rem(i + 1, slabs)
     before = lax.rem(i + slabs - 1, slabs)
@@ -67,6 +73,45 @@
             barrier, inc=1, device_id=(before, lax.rem(d + o, bands)), device_id_type=MESH
         )
     pl.semaphore_wait(barrier, 2 * bands - 1)
+    frames, rows = pixel_ref.shape[:2]
+    rim_t, rim_h = WT - 1, WH - 1
+    next_band = lax.rem(d + 1, bands)
+    last_rows = pl.ds(rows - rim_h, rim_h)
+    last_frames = pl.ds(frames - rim_t, rim_t)
+    halos = []
+    for m, (source, target, device) in enumerate(
+        (
+            (pixel_ref.at[:, last_rows], row_ref, (i, next_band)),
+            (pixel_ref.at[last_frames], frame_ref, (after, d)),
+            (pixel_ref.at[last_frames, last_rows], corner_ref, (after, next_band)),
+        )
+    ):
+        copy = pltpu.make_async_remote_copy(
+            src_ref=source,
+            dst_ref=target,
+            send_sem=halo_send.at[m],
+            recv_sem=halo_recv.at[m],
+            device_id=device,
+            device_id_type=MESH,
+        )
+        copy.start()
+        halos.append(copy)
+    slots, width = visible_ref.shape[1:]
+    parts = TILE // slots
+    chunk = width // parts
+    slot_of = lax.broadcasted_iota(jnp.int32, (TILE, LANES), 0) % slots
+    for e in range(bands):
+        values = visible_ref[e].astype(F32)
+        values = jnp.concatenate(
+            [values[:, j * chunk : (j + 1) * chunk] for j in range(parts)], axis=0
+        ).astype(BF16)
+        index = jnp.full((TILE, LANES), slot_ref[e, 0], jnp.int32)
+        for c in range(1, slots):
+            index = jnp.where(slot_of == c, slot_ref[e, c], index)
+        index = index.astype(F32).astype(BF16)
+        for at, k in ((e, 1), ((e + 1) % bands, 0)):
+            x_ref[at, k, :, :chunk] = values
+            x_ref[at, k, :, chunk:] = index
     copies = []
     for q, slab in ((1, after), (0, i)):
         for o in range(1 - q, bands):
@@ -94,10 +139,12 @@
         )
         arriving.wait_recv()
         copy.wait_send()
+    for copy in halos:
+        copy.wait()
 
 
 def collect_kernel(
-    slabs, bands, x_ref, sum_ref, out_ref, total_ref,
+    slabs, bands, grad_scale, x_ref, sum_ref, out_ref, total_ref,
     got, row_sums, slab_sums, mine,
     send_sem, recv_sem, row_send, row_recv, slab_send, slab_recv,
 ):
@@ -190,6 +237,10 @@
         f = (e + 1) % bands
         value = got[e, 1].astype(F32) + got[f, 0].astype(F32)
         value = value + got[bands + e, 1].astype(F32) + got[bands + f, 0].astype(F32)
+        slots = out_ref.shape[1]
+        value = jnp.concatenate(
+            [value[j * slots : (j + 1) * slots] for j in range(TILE // slots)], axis=1
+        )
         out_ref[e] = value.astype(BF16)
     for o, copy in enumerate(sums, 1):
         s = lax.rem(i + slabs - o, slabs)
@@ -205,15 +256,17 @@
     total = slab_sums[0]
     for s in range(1, slabs):
         total = total + slab_sums[s]
-    total_ref[...] = total
+    total = total * grad_scale
+    for j in range(total.shape[0]):
+        total_ref[:, j * LANES : (j + 1) * LANES] = total[j : j + 1]
 
 
 def block_kernel(
-    slots, grid,
-    shift_ref, recv_ref, token_ref, mask_ref, pos_t_ref, pos_h_ref, pos_c_ref,
-    w_qkv_ref, w_out_ref, w_head_ref, own_ref, rows_ref, frames_ref, corner_ref,
+    slots, grid, slabs, bands,
+    shift_ref, recv_ref, mask_ref,
+    w_qkv_hbm, w_out_hbm, w_head_hbm, own_ref, rows_ref, frames_ref, corner_ref,
     picked_ref, sum_ref,
-    joined, pix, probs, mixed, d_qkv,
+    joined, pix, probs, mixed, d_qkv, w_qkv_ref, w_out_ref, w_head_ref, sems,
 ):
     frames, rows, columns = grid
     groups = columns // WW
@@ -225,12 +278,65 @@
     total_rows = recv_ref.shape[0]
     rim_t, rim_h = WT - 1, WH - 1
 
+    inner_rows, outer_rows = pl.ds(rim_h, rows), pl.ds(0, rim_h)
+    inner_frames, outer_frames = pl.ds(rim_t, frames), pl.ds(0, rim_t)
+    loads = [
+        pltpu.make_async_copy(source, target, sems.at[m])
+        for m, (source, target) in enumerate(
+            (
+                (w_qkv_hbm, w_qkv_ref),
+                (w_out_hbm, w_out_ref),
+                (own_ref, joined.at[inner_frames, inner_rows]),
+                (rows_ref, joined.at[inner_frames, outer_rows]),
+                (frames_ref, joined.at[outer_frames, inner_rows]),
+                (corner_ref, joined.at[outer_frames, outer_rows]),
+                (w_head_hbm, w_head_ref),
+            )
+        )
+    ]
+    for load in loads:
+        load.start()
+
+    n = lax.broadcasted_iota(jnp.int32, (1, tokens), 1)
+    group = n // (WW * WH * WT) % groups
+    t_shift = h_shift = jnp.zeros((1, tokens), jnp.int32)
+    for a in range(groups):
+        t_shift = jnp.where(group == a, shift_ref[0, a], t_shift)
+        h_shift = jnp.where(group == a, shift_ref[1, a], h_shift)
+    per_pair = WW * WH * WT * groups
+    t = n // (per_pair * (rows // WH)) * WT + n // (WW * WH) % WT - t_shift
+    h = n // per_pair % (rows // WH) * WH + n // WW % WH - h_shift
+    local = jnp.where(t < 0, t + frames, t) * rows + jnp.where(h < 0, h + rows, h)
+    local = local * columns + group * WW + n % WW
+    lines = [
+        jnp.where(((t < 0) == (q == 1)) & ((h < 0) == (k == 0)), local, -2).astype(F32)
+        for q in range(2)
+        for k in range(2)
+    ]
+    quarter = width // 4
+    rest = (width - quarter) // 2
+    i, d = lax.axis_index("tm"), lax.axis_index("row")
+    t_count, h_count = frames * slabs, rows * bands
+
+    def table(count, total, base, shifts, channels):
+        row = lax.broadcasted_iota(jnp.int32, (groups * count, channels), 0)
+        at = base + row % count + total
+        for a in range(groups):
+            at = jnp.where(row // count == a, at - shift_ref[shifts, a], at)
+        at = jnp.where(at >= total, at - total, at)
+        return sinusoid(at.astype(F32), channels)
+
+    pos_t = table(frames, t_count, i * frames, 0, quarter)
+    pos_h = table(rows, h_count, d * rows, 1, rest)
+    last = width - quarter - rest
+    pos_c = sinusoid(lax.broadcasted_iota(jnp.int32, (columns, last), 0).astype(F32), last)
+
     index = recv_ref[:, chunk:].astype(F32)
     index = jnp.concatenate([index] * (tokens // LANES), axis=1)
     pieces = []
     for block in range(total_rows // TILE):
         q = block // (total_rows // TILE // 2)
-        line = token_ref[2 * q + block % 2 : 2 * q + block % 2 + 1, :]
+        line = lines[2 * q + block % 2]
         pieces.append(jnp.broadcast_to(line, (TILE, tokens)))
     hit = (index == jnp.concatenate(pieces, axis=0)).astype(F32)
     part_of = lax.broadcasted_iota(jnp.int32, (total_rows, tokens), 0) // slots % parts
@@ -263,9 +369,9 @@
         pieces.append(
             jnp.concatenate(
                 [
-                    jnp.broadcast_to(pos_t_ref[t_line : t_line + 1], (WW, pos_t_ref.shape[1])),
-                    jnp.broadcast_to(pos_h_ref[h_line : h_line + 1], (WW, pos_h_ref.shape[1])),
-                    pos_c_ref[g * WW : (g + 1) * WW],
+                    jnp.broadcast_to(pos_t[t_line : t_line + 1], (WW, quarter)),
+                    jnp.broadcast_to(pos_h[h_line : h_line + 1], (WW, rest)),
+                    pos_c[g * WW : (g + 1) * WW],
                 ],
                 axis=1,
             )
@@ -273,6 +379,7 @@
     embedded = (start + jnp.concatenate(pieces, axis=0)).astype(BF16).astype(F32)
 
     normed, scale = norm_parts(embedded)
+    loads[0].wait()
     qkv = nn_dot(normed.astype(BF16), w_qkv_ref[...]).astype(BF16)
 
     window = WT * WH * WW
@@ -285,6 +392,11 @@
     lane = lax.broadcasted_iota(jnp.int32, (span, pair), 1) // head_dim
     zero = jnp.zeros((span, pair), BF16)
 
+    def halves(values):
+        return jnp.concatenate(
+            [jnp.where(lane == 0, values, zero), jnp.where(lane == 1, values, zero)], axis=0
+        )
+
     def block_of(values, b, at):
         return values[b * span : (b + 1) * span, at : at + pair]
 
@@ -293,33 +405,26 @@
             q = block_of(qkv, b, p * pair)
             k = block_of(qkv, b, width + p * pair)
             v = block_of(qkv, b, 2 * width + p * pair)
-            out = None
-            for h in range(2):
-                scores = nt_dot(q, jnp.where(lane == h, k, zero)) * head_dim ** (-0.5)
-                scores = jnp.where(same, scores, -jnp.inf)
-                weights = jnp.exp(scores - jnp.max(scores, axis=-1, keepdims=True))
-                weights = weights / jnp.sum(weights, axis=-1, keepdims=True)
-                probs[(b * HEADS // 2 + p) * 2 + h] = weights
-                part = nn_dot(weights.astype(BF16), jnp.where(lane == h, v, zero))
-                out = part if out is None else out + part
+            scores = nt_dot(q, halves(k)) * head_dim ** (-0.5)
+            both = []
+            for m in range(2):
+                part = jnp.where(same, scores[:, m * span : (m + 1) * span], -jnp.inf)
+                weights = jnp.exp(part - jnp.max(part, axis=-1, keepdims=True))
+                both.append(weights * (1.0 / jnp.sum(weights, axis=-1, keepdims=True)))
+            weights = jnp.concatenate(both, axis=1)
+            probs[b * HEADS // 2 + p] = weights
+            out = nn_dot(weights.astype(BF16), halves(v))
             mixed[b * span : (b + 1) * span, p * pair : (p + 1) * pair] = out.astype(BF16)
+    loads[1].wait()
     attn = nn_dot(mixed[...], w_out_ref[...]).astype(BF16)
     residual = embedded + attn.astype(F32)
 
-    for t in range(frames):
-        for h in range(rows):
-            joined[(t + rim_t) * (rows + rim_h) + h + rim_h] = own_ref[t, h]
-        for h in range(rim_h):
-            joined[(t + rim_t) * (rows + rim_h) + h] = rows_ref[t, h]
-    for t in range(rim_t):
-        for h in range(rows):
-            joined[t * (rows + rim_h) + h + rim_h] = frames_ref[t, h]
-        for h in range(rim_h):
-            joined[t * (rows + rim_h) + h] = corner_ref[t, h]
+    for load in loads[2:6]:
+        load.wait()
     for n, (fw, hw, g, ft, r) in enumerate(order):
         t = fw * WT + ft + rim_t - shift_ref[0, g]
         h = hw * WH + r + rim_h - shift_ref[1, g]
-        pix[n * WW : (n + 1) * WW, :] = joined[t * (rows + rim_h) + h][
+        pix[n * WW : (n + 1) * WW, :] = joined[t, h][
             g * WW : (g + 1) * WW, :
         ].astype(F32)
     group_size = pix.shape[1] // 3
@@ -328,10 +433,11 @@
         raw = pix[:, c * group_size : (c + 1) * group_size]
         center = raw - jnp.mean(raw, axis=-1, keepdims=True)
         spread = jnp.sqrt(jnp.sum(center * center, axis=-1, keepdims=True) / (group_size - 1))
-        targets.append(center / (spread + 1e-06))
+        targets.append(center * (1.0 / (spread + 1e-06)))
     target = jnp.concatenate(targets, axis=1)
 
     normed_out, scale_out = norm_parts(residual)
+    loads[6].wait()
     predicted = nn_dot(normed_out.astype(BF16), w_head_ref[...])
     errors = (predicted - target) * masked
     d_normed_out = nt_dot(errors.astype(BF16), w_head_ref[...]).astype(BF16).astype(F32)
@@ -344,23 +450,20 @@
             k = block_of(qkv, b, width + p * pair)
             v = block_of(qkv, b, 2 * width + p * pair)
             d_out = block_of(d_mixed, b, p * pair)
-            dq = dk = dv = None
-            for h in range(2):
-                mine = lane == h
-                weights = probs[(b * HEADS // 2 + p) * 2 + h]
-                d_weights = nt_dot(d_out, jnp.where(mine, v, zero)).astype(BF16).astype(F32)
-                inner = jnp.sum(weights * d_weights, axis=-1, keepdims=True)
-                d_scores = weights * (d_weights - inner) * head_dim ** (-0.5)
-                d_scores = d_scores.astype(BF16)
-                terms = (
-                    nn_dot(d_scores, jnp.where(mine, k, zero)),
-                    tn_dot(d_scores, jnp.where(mine, q, zero)),
-                    tn_dot(weights.astype(BF16), jnp.where(mine, d_out, zero)),
-                )
-                if h == 0:
-                    dq, dk, dv = terms
-                else:
-                    dq, dk, dv = dq + terms[0], dk + terms[1], dv + terms[2]
+            weights = probs[b * HEADS // 2 + p]
+            d_weights = nt_dot(d_out, halves(v)).astype(BF16).astype(F32)
+            both = []
+            for m in range(2):
+                w = weights[:, m * span : (m + 1) * span]
+                dw = d_weights[:, m * span : (m + 1) * span]
+                inner = jnp.sum(w * dw, axis=-1, keepdims=True)
+                both.append(w * (dw - inner) * head_dim ** (-0.5))
+            d_scores = jnp.concatenate(both, axis=1).astype(BF16)
+            dq = nn_dot(d_scores, halves(k))
+            dk = tn_dot(d_scores, q)
+            dv = tn_dot(weights.astype(BF16), d_out)
+            dk = jnp.where(lane == 0, dk[:span], dk[span:])
+            dv = jnp.where(lane == 0, dv[:span], dv[span:])
             for m, value in enumerate((dq, dk, dv)):
                 at = m * width + p * pair
                 d_qkv[b * span : (b + 1) * span, at : at + pair] = value.astype(BF16)
@@ -386,91 +489,56 @@
     tokens = frames * rows * columns
     bands, slots = slot_pos.shape[2:]
     slabs = lax.axis_size("tm")
-    groups = columns // WW
     parts = TILE // slots
     chunk = width // parts
     rim_t, rim_h = WT - 1, WH - 1
-    i, d = lax.axis_index("tm"), lax.axis_index("row")
     vmem = pl.BlockSpec(memory_space=pltpu.VMEM)
-
-    both = ("tm", "row")
-    slab_ring = [(a, (a + 1) % slabs) for a in range(slabs)]
-    band_ring = [(a, (a + 1) % bands) for a in range(bands)]
-    corner_ring = [
-        (a * bands + b, (a + 1) % slabs * bands + (b + 1) % bands)
-        for a in range(slabs)
-        for b in range(bands)
-    ]
-    row_halo = lax.ppermute(pixels[:, rows - rim_h :], "row", band_ring)
-    frame_halo = lax.ppermute(pixels[frames - rim_t :], "tm", slab_ring)
-    corner_halo = lax.ppermute(pixels[frames - rim_t :, rows - rim_h :], both, corner_ring)
-
-    packed = visible.reshape(bands, slots, parts, chunk).transpose(0, 2, 1, 3)
-    packed = packed.reshape(bands, TILE, chunk)
-    index = jnp.broadcast_to(
-        slot_pos.reshape(bands, 1, slots, 1), (bands, parts, slots, LANES)
-    ).reshape(bands, TILE, LANES)
-    packed = jnp.concatenate([packed, index.astype(BF16)], axis=-1)
-    packed = jnp.stack([jnp.roll(packed, 1, axis=0), packed], axis=1)
+    smem = pl.BlockSpec(memory_space=pltpu.SMEM)
+    anywhere = pl.BlockSpec(memory_space=pl.ANY)
     wide = chunk + LANES
-    received = pl.pallas_call(
+    received, row_halo, frame_halo, corner_halo = pl.pallas_call(
         functools.partial(spread_kernel, slabs, bands),
-        out_shape=jax.ShapeDtypeStruct((2 * bands, 2, TILE, wide), BF16),
-        in_specs=[vmem],
-        out_specs=vmem,
+        out_shape=(
+            jax.ShapeDtypeStruct((2 * bands, 2, TILE, wide), BF16),
+            jax.ShapeDtypeStruct((frames, rim_h, columns, pixel_count), BF16),
+            jax.ShapeDtypeStruct((rim_t, rows, columns, pixel_count), BF16),
+            jax.ShapeDtypeStruct((rim_t, rim_h, columns, pixel_count), BF16),
+        ),
+        in_specs=[smem, vmem, anywhere],
+        out_specs=(vmem, anywhere, anywhere, anywhere),
         scratch_shapes=[
+            pltpu.VMEM((bands, 2, TILE, wide), BF16),
             pltpu.SemaphoreType.DMA((2 * bands,)),
             pltpu.SemaphoreType.DMA((2 * bands,)),
+            pltpu.SemaphoreType.DMA((3,)),
+            pltpu.SemaphoreType.DMA((3,)),
         ],
         compiler_params=pltpu.CompilerParams(collective_id=0, has_side_effects=True),
         name="spread",
-    )(packed)
-
-    n = jnp.arange(tokens, dtype=jnp.int32)
-    column = n % WW
-    r = n // WW % WH
-    ft = n // (WW * WH) % WT
-    g = n // (WW * WH * WT) % groups
-    hw = n // (WW * WH * WT * groups) % (rows // WH)
-    fw = n // (WW * WH * WT * groups * (rows // WH))
-    t_shift = sum(jnp.where(g == a, window_shift[0, a], 0) for a in range(groups))
-    h_shift = sum(jnp.where(g == a, window_shift[1, a], 0) for a in range(groups))
-    t = fw * WT + ft - t_shift
-    h = hw * WH + r - h_shift
-    local = (t % frames * rows + h % rows) * columns + g * WW + column
-    token_index = jnp.stack(
-        [
-            jnp.where(((t < 0) == (q == 1)) & ((h < 0) == (k == 0)), local, -2)
-            for q in range(2)
-            for k in range(2)
-        ]
-    ).astype(F32)
-    quarter = width // 4
-    rest = (width - quarter) // 2
-    t_all = (i * frames + jnp.arange(frames) - window_shift[0][:, None]) % (frames * slabs)
-    h_all = (d * rows + jnp.arange(rows) - window_shift[1][:, None]) % (rows * bands)
-    pos_t = sinusoid(t_all.reshape(-1), quarter)
-    pos_h = sinusoid(h_all.reshape(-1), rest)
-    pos_c = sinusoid(jnp.arange(columns), width - quarter - rest)
+    )(slot_pos.reshape(bands, slots), visible.reshape(bands, slots, width), pixels)
 
     total_rows = 2 * bands * 2 * TILE
     flops = 4 * tokens * width * (w_qkv.shape[1] + width + pixel_count)
     picked, partial_sum = pl.pallas_call(
-        functools.partial(block_kernel, slots, (frames, rows, columns)),
+        functools.partial(block_kernel, slots, (frames, rows, columns), slabs, bands),
         out_shape=(
             jax.ShapeDtypeStruct((total_rows, chunk), BF16),
             jax.ShapeDtypeStruct((width // LANES, LANES), F32),
         ),
-        in_specs=[pl.BlockSpec(memory_space=pltpu.SMEM)] + [vmem] * 13,
+        in_specs=[smem, vmem, vmem] + [anywhere] * 7,
         out_specs=(vmem, vmem),
         scratch_shapes=[
-            pltpu.VMEM(((frames + rim_t) * (rows + rim_h), columns, pixel_count), BF16),
+            pltpu.VMEM((frames + rim_t, rows + rim_h, columns, pixel_count), BF16),
             pltpu.VMEM((tokens, pixel_count), F32),
             pltpu.VMEM(
-                (HEADS * tokens // (2 * WT * WH * WW), 2 * WT * WH * WW, 2 * WT * WH * WW), F32
+                (HEADS * tokens // (4 * WT * WH * WW), 2 * WT * WH * WW, 4 * WT * WH * WW), F32
             ),
             pltpu.VMEM((tokens, width), BF16),
             pltpu.VMEM((tokens, 3 * width), BF16),
+            pltpu.VMEM(w_qkv.shape, BF16),
+            pltpu.VMEM(w_out.shape, BF16),
+            pltpu.VMEM(w_head.shape, BF16),
+            pltpu.SemaphoreType.DMA((7,)),
         ],
         compiler_params=pltpu.CompilerParams(vmem_limit_bytes=56 * 2**20),
         cost_estimate=pl.CostEstimate(
@@ -478,16 +546,16 @@
         ),
         name="block",
     )(
-        window_shift, received.reshape(total_rows, wide), token_index, mask_token[None, :],
-        pos_t, pos_h, pos_c, w_qkv, w_out, w_head, pixels, row_halo, frame_halo, corner_halo,
+        window_shift, received.reshape(total_rows, wide), mask_token[None, :],
+        w_qkv, w_out, w_head, pixels, row_halo, frame_halo, corner_halo,
     )
 
     lines = width // LANES
     returned, total = pl.pallas_call(
-        functools.partial(collect_kernel, slabs, bands),
+        functools.partial(collect_kernel, slabs, bands, (tokens * slabs * bands) ** (-0.5)),
         out_shape=(
-            jax.ShapeDtypeStruct((bands, TILE, chunk), BF16),
-            jax.ShapeDtypeStruct((lines, LANES), F32),
+            jax.ShapeDtypeStruct((bands, slots, width), BF16),
+            jax.ShapeDtypeStruct((1, width), F32),
         ),
         in_specs=[vmem, vmem],
         out_specs=(vmem, vmem),
@@ -506,9 +574,7 @@
         compiler_params=pltpu.CompilerParams(collective_id=1, has_side_effects=True),
         name="collect",
     )(picked.reshape(2 * bands, 2, TILE, chunk), partial_sum)
-    d_visible = returned.reshape(bands, parts, slots, chunk).transpose(0, 2, 1, 3)
-    grad_scale = (tokens * slabs * bands) ** (-0.5)
-    return d_visible.reshape(visible.shape), total.reshape(width) * grad_scale
+    return returned.reshape(visible.shape), total.reshape(width)
 
 
 def solution(mesh):

time: 76 us -> 59.1 us (0.78)
  other arithmetic: 10.9 us -> 0 us
  starting transfers between devices: 5.69 us -> 0 us
  local copies, waits for them, and re-layouts: 9.33 us -> 5.39 us
  Pallas kernels: 48.8 us -> 52.7 us
    pallas_call x1, Pallas kernels: 12.6 us -> 22.1 us  [per_device(): pl.pallas_call(functools.partial(spread_kernel, slabs, bands), out_shape=...]
    pallas_call x1, Pallas kernels: 25.2 us -> 19.2 us  [per_device(): pl.pallas_call(functools.partial(block_kernel, slots, (frames, rows, colu...]
    ppermute x3 -> x0, starting transfers between devices: 5.69 us -> none  [the longest x1 2.64 us: per_device(): frame_halo = lax.ppermute(pixels[frames - rim_t:], 'tm', slab_ring)]
    select_n x2 -> x0, other arithmetic: 5.11 us -> none  [per_device(): jnp.where(((t < 0) == (q == 1)) & ((h < 0) == (k == 0)), local, -2)]
    slice x4 -> x0, local copies, waits for them, and re-layouts: 4.39 us -> none  [the longest x1 1.42 us: per_device(): window_shift[1, a]]
    concatenate x5 -> x0, other arithmetic: 1.97 us -> none  [the longest x3 1.95 us: sinusoid(): return jnp.concatenate([jnp.sin(angles), jnp.cos(angles)], axis=-1)]
    unnamed x8 -> x2, local copies, waits for them, and re-layouts: 0.9 us -> 2.77 us
    convert_element_type x5 -> x0, other arithmetic: 1.32 us -> none  [the longest x1 0.69 us: per_device(): packed = jnp.concatenate([packed, index.astype(BF16)], axis=-1)]
  transfers between devices with their start and end apart: 3 -> 0, of which waited for: 0 -> 0; matrix products, arithmetic and copies ran while one was open for 20% -> 0% of each run, Pallas kernels for 17% -> 0%
where the time goes in v2:
time: 59.1 us; the launch traced here: 58.8 us
  Pallas kernels  52.7 us (89%)
  local copies, waits for them, and re-layouts  5.39 us (9%)
  between operations  0.65 us (1%)
    pallas_call x1, Pallas kernels, per_device(): pl.pallas_call(functools.partial(spread_kernel, slabs, bands), out_shape=...  22.1 us
    pallas_call x1, Pallas kernels, per_device(): pl.pallas_call(functools.partial(block_kernel, slots, (frames, rows, colu...  19.2 us
    pallas_call x1, Pallas kernels, per_device(): pl.pallas_call(functools.partial(collect_kernel, slabs, bands, (tokens *...  11.5 us
    unnamed x2, local copies, waits for them, and re-layouts  2.77 us
    reshape x1, local copies, waits for them, and re-layouts, per_device(): slot_pos.reshape(bands, slots)  1.35 us
    broadcast_in_dim x1, local copies, waits for them, and re-layouts, per_device(): mask_token[None, :]  1.28 us

profile of v2, /device:TPU:0, one launch (start us, length us, event | category | flops | bytes accessed | tf_op | source)
XLA Modules:
  0.0 58.8 jit_solution(7563089357945020772)
XLA Ops:
  0.6 1.3 %copy.10.slot_ref = s32[8,4]{1,0:T(8,128)} copy(s32[8,4]{0,1:T(4,128)} %bitcast.10) | data formatting | bytes 256 | tf_op jit(solution)/shard_map/reshape | solution.py:518
  2.0 1.3 %broadcast_in_dim.3.mask_ref = bf16[1,1024]{1,0:T(2,128)(2,1)} reshape(bf16[1024]{0:T(1024)(128)(2,1)} %param.11) | data formatting | bytes 4096 | tf_op jit(solution)/shard_map/broadcast_in_dim | solution.py:549
  3.3 22.1 %spread.1 = (bf16[16,2,16,384]{3,2,1,0:T(8,128)(2,1)}, bf16[4,3,16,1536]{3,2,1,0:T(8,128)(2,1)}, bf16[1,4,16,1536]{3,2,1,0:T(8,128)(2,1)}, bf16[1,3,16,1536]{3,2,1,0:T(8,128)(2,1)}) custom-call(s32[8,4]{1,0:T(8,128)} %copy.10.slot_ref, bf16[8,4,1024]{2,1,0:T(4,128)(2,1)} %bitcast.8, bf16[4,4,16,1536]{3,2,1,0:T(8,128)(2,1)} %own_ref.1), custom_call_target="tpu_custom_call" | custom-call | tf_op jit(solution)/shard_map/spread/pallas_call | solution.py:499
  25.4 19.2 %block.1 = (bf16[512,256]{1,0:T(8,128)(2,1)}, f32[8,128]{1,0:T(8,128)}) custom-call(s32[2,2]{1,0:T(2,128)} %shift_ref.1, bf16[512,384]{1,0:T(8,128)(2,1)} %bitcast.11, bf16[1,1024]{1,0:T(2,128)(2,1)} %broadcast_in_dim.3.mask_ref, bf16[1024,3072]{1,0:T(8,128)(2,1)} %w_qkv_hbm.1, bf16[1024,1024]{1,0:T(8,128)(2,1)} %w_out_hbm.1, bf16[1024,1536]{1,0:T(8,128)(2,1)} %w_head_hbm.1, ...), custom_call_target="tpu_custom_call" | custom-call | flops 5905580032 | bytes 16777216 | tf_op jit(solution)/shard_map/block/pallas_call | solution.py:522
  44.5 11.5 %collect.1 = (bf16[8,4,1024]{2,1,0:T(4,128)(2,1)}, f32[1,1024]{1,0:T(1,128)}) custom-call(bf16[16,2,16,256]{3,2,1,0:T(8,128)(2,1)} %bitcast.6, f32[8,128]{1,0:T(8,128)} %get-tuple-element.15.sum_ref), custom_call_target="tpu_custom_call" | custom-call | tf_op jit(solution)/shard_map/collect/pallas_call | solution.py:554
  56.0 1.5 %copy.13 = bf16[1,1,8,4,1024]{4,3,2,1,0:T(4,128)(2,1)} copy(bf16[1,1,8,4,1024]{4,3,2,1,0:T(4,128)(2,1)} %bitcast.7) | data formatting | bytes 131072
  57.5 1.3 %copy.14 = f32[1024]{0:T(1024)} copy(f32[1024]{0:T(1024)} %bitcast.9) | data formatting | bytes 8192

commit v3 on v2

--- a/solution.py
+++ b/solution.py
@@ -55,9 +55,8 @@
     )
 
 
-def spread_kernel(
-    slabs, bands, slot_ref, visible_ref, pixel_ref,
-    out_ref, row_ref, frame_ref, corner_ref,
+def exchange(
+    slabs, bands, slot_ref, visible_ref, pixel_ref, out_ref, joined,
     x_ref, send_sem, recv_sem, halo_send, halo_recv,
 ):
     i, d = lax.axis_index("tm"), lax.axis_index("row")
@@ -78,12 +77,18 @@
     next_band = lax.rem(d + 1, bands)
     last_rows = pl.ds(rows - rim_h, rim_h)
     last_frames = pl.ds(frames - rim_t, rim_t)
+    inner_rows, outer_rows = pl.ds(rim_h, rows), pl.ds(0, rim_h)
+    inner_frames, outer_frames = pl.ds(rim_t, frames), pl.ds(0, rim_t)
     halos = []
     for m, (source, target, device) in enumerate(
         (
-            (pixel_ref.at[:, last_rows], row_ref, (i, next_band)),
-            (pixel_ref.at[last_frames], frame_ref, (after, d)),
-            (pixel_ref.at[last_frames, last_rows], corner_ref, (after, next_band)),
+            (pixel_ref.at[:, last_rows], joined.at[inner_frames, outer_rows], (i, next_band)),
+            (pixel_ref.at[last_frames], joined.at[outer_frames, inner_rows], (after, d)),
+            (
+                pixel_ref.at[last_frames, last_rows],
+                joined.at[outer_frames, outer_rows],
+                (after, next_band),
+            ),
         )
     ):
         copy = pltpu.make_async_remote_copy(
@@ -96,18 +101,18 @@
         )
         copy.start()
         halos.append(copy)
-    slots, width = visible_ref.shape[1:]
+    slots, width = visible_ref.shape[3:]
     parts = TILE // slots
     chunk = width // parts
     slot_of = lax.broadcasted_iota(jnp.int32, (TILE, LANES), 0) % slots
     for e in range(bands):
-        values = visible_ref[e].astype(F32)
+        values = visible_ref[0, 0, e].astype(F32)
         values = jnp.concatenate(
             [values[:, j * chunk : (j + 1) * chunk] for j in range(parts)], axis=0
         ).astype(BF16)
-        index = jnp.full((TILE, LANES), slot_ref[e, 0], jnp.int32)
+        index = jnp.full((TILE, LANES), slot_ref[0, 0, e, 0], jnp.int32)
         for c in range(1, slots):
-            index = jnp.where(slot_of == c, slot_ref[e, c], index)
+            index = jnp.where(slot_of == c, slot_ref[0, 0, e, c], index)
         index = index.astype(F32).astype(BF16)
         for at, k in ((e, 1), ((e + 1) % bands, 0)):
             x_ref[at, k, :, :chunk] = values
@@ -139,8 +144,7 @@
         )
         arriving.wait_recv()
         copy.wait_send()
-    for copy in halos:
-        copy.wait()
+    return halos
 
 
 def collect_kernel(
@@ -263,39 +267,39 @@
 
 def block_kernel(
     slots, grid, slabs, bands,
-    shift_ref, recv_ref, mask_ref,
-    w_qkv_hbm, w_out_hbm, w_head_hbm, own_ref, rows_ref, frames_ref, corner_ref,
+    slot_ref, shift_ref, visible_ref, mask_ref,
+    w_qkv_hbm, w_out_hbm, w_head_hbm, own_ref,
     picked_ref, sum_ref,
     joined, pix, probs, mixed, d_qkv, w_qkv_ref, w_out_ref, w_head_ref, sems,
+    got_ref, x_ref, send_sem, recv_sem, halo_send, halo_recv,
 ):
     frames, rows, columns = grid
     groups = columns // WW
     tokens = frames * rows * columns
-    width = mask_ref.shape[1]
+    width = mask_ref.shape[0]
     head_dim = width // HEADS
     parts = TILE // slots
     chunk = width // parts
-    total_rows = recv_ref.shape[0]
+    total_rows = 2 * bands * 2 * TILE
     rim_t, rim_h = WT - 1, WH - 1
 
-    inner_rows, outer_rows = pl.ds(rim_h, rows), pl.ds(0, rim_h)
-    inner_frames, outer_frames = pl.ds(rim_t, frames), pl.ds(0, rim_t)
     loads = [
         pltpu.make_async_copy(source, target, sems.at[m])
         for m, (source, target) in enumerate(
             (
                 (w_qkv_hbm, w_qkv_ref),
                 (w_out_hbm, w_out_ref),
-                (own_ref, joined.at[inner_frames, inner_rows]),
-                (rows_ref, joined.at[inner_frames, outer_rows]),
-                (frames_ref, joined.at[outer_frames, inner_rows]),
-                (corner_ref, joined.at[outer_frames, outer_rows]),
+                (own_ref, joined.at[pl.ds(rim_t, frames), pl.ds(rim_h, rows)]),
                 (w_head_hbm, w_head_ref),
             )
         )
     ]
     for load in loads:
         load.start()
+    halos = exchange(
+        slabs, bands, slot_ref, visible_ref, own_ref, got_ref, joined,
+        x_ref, send_sem, recv_sem, halo_send, halo_recv,
+    )
 
     n = lax.broadcasted_iota(jnp.int32, (1, tokens), 1)
     group = n // (WW * WH * WT) % groups
@@ -331,7 +335,8 @@
     last = width - quarter - rest
     pos_c = sinusoid(lax.broadcasted_iota(jnp.int32, (columns, last), 0).astype(F32), last)
 
-    index = recv_ref[:, chunk:].astype(F32)
+    received = got_ref[...].reshape(total_rows, chunk + LANES)
+    index = received[:, chunk:].astype(F32)
     index = jnp.concatenate([index] * (tokens // LANES), axis=1)
     pieces = []
     for block in range(total_rows // TILE):
@@ -344,7 +349,7 @@
     hit_t = hit.T
     seen = jnp.max(hit_t, axis=1, keepdims=True)
     masked = 1.0 - seen
-    packed_rows = recv_ref[:, :chunk]
+    packed_rows = received[:, :chunk]
     start = jnp.concatenate(
         [
             nn_dot(jnp.where(part_of_t == j, hit_t, 0.0).astype(BF16), packed_rows)
@@ -352,7 +357,7 @@
         ],
         axis=1,
     )
-    start = jnp.where(seen > 0, start, mask_ref[...].astype(F32))
+    start = jnp.where(seen > 0, start, mask_ref[...].astype(F32)[None, :])
 
     order = [
         (fw, hw, g, ft, r)
@@ -419,8 +424,9 @@
     attn = nn_dot(mixed[...], w_out_ref[...]).astype(BF16)
     residual = embedded + attn.astype(F32)
 
-    for load in loads[2:6]:
-        load.wait()
+    loads[2].wait()
+    for copy in halos:
+        copy.wait()
     for n, (fw, hw, g, ft, r) in enumerate(order):
         t = fw * WT + ft + rim_t - shift_ref[0, g]
         h = hw * WH + r + rim_h - shift_ref[1, g]
@@ -437,7 +443,7 @@
     target = jnp.concatenate(targets, axis=1)
 
     normed_out, scale_out = norm_parts(residual)
-    loads[6].wait()
+    loads[3].wait()
     predicted = nn_dot(normed_out.astype(BF16), w_head_ref[...])
     errors = (predicted - target) * masked
     d_normed_out = nt_dot(errors.astype(BF16), w_head_ref[...]).astype(BF16).astype(F32)
@@ -496,27 +502,6 @@
     smem = pl.BlockSpec(memory_space=pltpu.SMEM)
     anywhere = pl.BlockSpec(memory_space=pl.ANY)
     wide = chunk + LANES
-    received, row_halo, frame_halo, corner_halo = pl.pallas_call(
-        functools.partial(spread_kernel, slabs, bands),
-        out_shape=(
-            jax.ShapeDtypeStruct((2 * bands, 2, TILE, wide), BF16),
-            jax.ShapeDtypeStruct((frames, rim_h, columns, pixel_count), BF16),
-            jax.ShapeDtypeStruct((rim_t, rows, columns, pixel_count), BF16),
-            jax.ShapeDtypeStruct((rim_t, rim_h, columns, pixel_count), BF16),
-        ),
-        in_specs=[smem, vmem, anywhere],
-        out_specs=(vmem, anywhere, anywhere, anywhere),
-        scratch_shapes=[
-            pltpu.VMEM((bands, 2, TILE, wide), BF16),
-            pltpu.SemaphoreType.DMA((2 * bands,)),
-            pltpu.SemaphoreType.DMA((2 * bands,)),
-            pltpu.SemaphoreType.DMA((3,)),
-            pltpu.SemaphoreType.DMA((3,)),
-        ],
-        compiler_params=pltpu.CompilerParams(collective_id=0, has_side_effects=True),
-        name="spread",
-    )(slot_pos.reshape(bands, slots), visible.reshape(bands, slots, width), pixels)
-
     total_rows = 2 * bands * 2 * TILE
     flops = 4 * tokens * width * (w_qkv.shape[1] + width + pixel_count)
     picked, partial_sum = pl.pallas_call(
@@ -525,7 +510,7 @@
             jax.ShapeDtypeStruct((total_rows, chunk), BF16),
             jax.ShapeDtypeStruct((width // LANES, LANES), F32),
         ),
-        in_specs=[smem, vmem, vmem] + [anywhere] * 7,
+        in_specs=[smem, smem, vmem, vmem] + [anywhere] * 4,
         out_specs=(vmem, vmem),
         scratch_shapes=[
             pltpu.VMEM((frames + rim_t, rows + rim_h, columns, pixel_count), BF16),
@@ -538,16 +523,23 @@
             pltpu.VMEM(w_qkv.shape, BF16),
             pltpu.VMEM(w_out.shape, BF16),
             pltpu.VMEM(w_head.shape, BF16),
-            pltpu.SemaphoreType.DMA((7,)),
+            pltpu.SemaphoreType.DMA((4,)),
+            pltpu.VMEM((2 * bands, 2, TILE, wide), BF16),
+            pltpu.VMEM((bands, 2, TILE, wide), BF16),
+            pltpu.SemaphoreType.DMA((2 * bands,)),
+            pltpu.SemaphoreType.DMA((2 * bands,)),
+            pltpu.SemaphoreType.DMA((3,)),
+            pltpu.SemaphoreType.DMA((3,)),
         ],
-        compiler_params=pltpu.CompilerParams(vmem_limit_bytes=56 * 2**20),
+        compiler_params=pltpu.CompilerParams(
+            collective_id=0, has_side_effects=True, vmem_limit_bytes=56 * 2**20
+        ),
         cost_estimate=pl.CostEstimate(
             flops=flops, bytes_accessed=16 * 2**20, transcendentals=HEADS * tokens * 128
         ),
         name="block",
     )(
-        window_shift, received.reshape(total_rows, wide), mask_token[None, :],
-        w_qkv, w_out, w_head, pixels, row_halo, frame_halo, corner_halo,
+        slot_pos, window_shift, visible, mask_token, w_qkv, w_out, w_head, pixels,
     )
 
     lines = width // LANES

time: 59.1 us -> 54 us (0.914)
  Pallas kernels: 52.7 us -> 49 us
  local copies, waits for them, and re-layouts: 5.39 us -> 4.11 us
    pallas_call x1 -> x0, Pallas kernels: 22.1 us -> none  [per_device(): pl.pallas_call(functools.partial(spread_kernel, slabs, bands), out_shape=...]
    pallas_call x1, Pallas kernels: 19.2 us -> 37.5 us  [per_device(): pl.pallas_call(functools.partial(block_kernel, slots, (frames, rows, colu...]
    reshape x1 -> x0, local copies, waits for them, and re-layouts: 1.35 us -> none  [per_device(): slot_pos.reshape(bands, slots)]
    unnamed x2 -> x3, local copies, waits for them, and re-layouts: 2.77 us -> 4.11 us
    broadcast_in_dim x1 -> x0, local copies, waits for them, and re-layouts: 1.28 us -> none  [per_device(): mask_token[None, :]]
where the time goes in v3:
time: 54 us; the launch traced here: 53.8 us
  Pallas kernels  49 us (91%)
  local copies, waits for them, and re-layouts  4.11 us (8%)
  between operations  0.65 us (1%)
    pallas_call x1, Pallas kernels, per_device(): pl.pallas_call(functools.partial(block_kernel, slots, (frames, rows, colu...  37.5 us
    pallas_call x1, Pallas kernels, per_device(): pl.pallas_call(functools.partial(collect_kernel, slabs, bands, (tokens *...  11.5 us
    unnamed x3, local copies, waits for them, and re-layouts  4.11 us

profile of v3, /device:TPU:0, one launch (start us, length us, event | category | flops | bytes accessed | tf_op | source)
XLA Modules:
  0.0 53.8 jit_solution(2158992065014433732)
XLA Ops:
  0.6 1.3 %copy.10.slot_ref = s32[1,1,8,4]{3,2,1,0:T(8,128)} copy(s32[1,1,8,4]{2,3,1,0:T(4,128)} %param.9) | data formatting | bytes 256 | tf_op args[1]
  2.0 37.5 %block.1 = (bf16[512,256]{1,0:T(8,128)(2,1)}, f32[8,128]{1,0:T(8,128)}) custom-call(s32[1,1,8,4]{3,2,1,0:T(8,128)} %copy.10.slot_ref, s32[2,2]{1,0:T(2,128)} %shift_ref.1, bf16[1,1,8,4,1024]{4,3,2,1,0:T(4,128)(2,1)} %visible_ref.1, bf16[1024]{0:T(1024)(128)(2,1)} %mask_ref.1, bf16[1024,3072]{1,0:T(8,128)(2,1)} %w_qkv_hbm.1, bf16[1024,1024]{1,0:T(8,128)(2,1)} %w_out_hbm.1, ...), custom_call_target="tpu_custom_call" | custom-call | flops 5905580032 | bytes 16777216 | tf_op jit(solution)/shard_map/block/pallas_call | solution.py:507
  39.5 11.5 %collect.1 = (bf16[8,4,1024]{2,1,0:T(4,128)(2,1)}, f32[1,1024]{1,0:T(1,128)}) custom-call(bf16[16,2,16,256]{3,2,1,0:T(8,128)(2,1)} %bitcast.3, f32[8,128]{1,0:T(8,128)} %get-tuple-element.7.sum_ref), custom_call_target="tpu_custom_call" | custom-call | tf_op jit(solution)/shard_map/collect/pallas_call | solution.py:546
  51.0 1.5 %copy.13 = bf16[1,1,8,4,1024]{4,3,2,1,0:T(4,128)(2,1)} copy(bf16[1,1,8,4,1024]{4,3,2,1,0:T(4,128)(2,1)} %bitcast.4) | data formatting | bytes 131072
  52.5 1.3 %copy.14 = f32[1024]{0:T(1024)} copy(f32[1024]{0:T(1024)} %bitcast.5) | data formatting | bytes 8192

commit v4 on v3

--- a/solution.py
+++ b/solution.py
@@ -77,30 +77,6 @@
     next_band = lax.rem(d + 1, bands)
     last_rows = pl.ds(rows - rim_h, rim_h)
     last_frames = pl.ds(frames - rim_t, rim_t)
-    inner_rows, outer_rows = pl.ds(rim_h, rows), pl.ds(0, rim_h)
-    inner_frames, outer_frames = pl.ds(rim_t, frames), pl.ds(0, rim_t)
-    halos = []
-    for m, (source, target, device) in enumerate(
-        (
-            (pixel_ref.at[:, last_rows], joined.at[inner_frames, outer_rows], (i, next_band)),
-            (pixel_ref.at[last_frames], joined.at[outer_frames, inner_rows], (after, d)),
-            (
-                pixel_ref.at[last_frames, last_rows],
-                joined.at[outer_frames, outer_rows],
-                (after, next_band),
-            ),
-        )
-    ):
-        copy = pltpu.make_async_remote_copy(
-            src_ref=source,
-            dst_ref=target,
-            send_sem=halo_send.at[m],
-            recv_sem=halo_recv.at[m],
-            device_id=device,
-            device_id_type=MESH,
-        )
-        copy.start()
-        halos.append(copy)
     slots, width = visible_ref.shape[3:]
     parts = TILE // slots
     chunk = width // parts
@@ -131,6 +107,30 @@
             )
             copy.start()
             copies.append((q, o, copy))
+    inner_rows, outer_rows = pl.ds(rim_h, rows), pl.ds(0, rim_h)
+    inner_frames, outer_frames = pl.ds(rim_t, frames), pl.ds(0, rim_t)
+    halos = []
+    for m, (source, target, device) in enumerate(
+        (
+            (pixel_ref.at[:, last_rows], joined.at[inner_frames, outer_rows], (i, next_band)),
+            (pixel_ref.at[last_frames], joined.at[outer_frames, inner_rows], (after, d)),
+            (
+                pixel_ref.at[last_frames, last_rows],
+                joined.at[outer_frames, outer_rows],
+                (after, next_band),
+            ),
+        )
+    ):
+        copy = pltpu.make_async_remote_copy(
+            src_ref=source,
+            dst_ref=target,
+            send_sem=halo_send.at[m],
+            recv_sem=halo_recv.at[m],
+            device_id=device,
+            device_id_type=MESH,
+        )
+        copy.start()
+        halos.append(copy)
     out_ref[d] = x_ref[d]
     for q, o, copy in copies:
         s = lax.rem(d + bands - o, bands)

time: 54 us -> 48.3 us (0.89)
  Pallas kernels: 49 us -> 43.3 us
    pallas_call x1, Pallas kernels: 37.5 us -> 32.3 us  [per_device(): pl.pallas_call(functools.partial(block_kernel, slots, (frames, rows, colu...]
where the time goes in v4:
time: 48.3 us; the launch traced here: 48.1 us
  Pallas kernels  43.3 us (90%)
  local copies, waits for them, and re-layouts  4.11 us (9%)
  between operations  0.65 us (1%)
    pallas_call x1, Pallas kernels, per_device(): pl.pallas_call(functools.partial(block_kernel, slots, (frames, rows, colu...  32.3 us
    pallas_call x1, Pallas kernels, per_device(): pl.pallas_call(functools.partial(collect_kernel, slabs, bands, (tokens *...  11 us
    unnamed x3, local copies, waits for them, and re-layouts  4.11 us

profile of v4, /device:TPU:0, one launch (start us, length us, event | category | flops | bytes accessed | tf_op | source)
XLA Modules:
  0.0 48.1 jit_solution(3328375255318309141)
XLA Ops:
  0.6 1.3 %copy.10.slot_ref = s32[1,1,8,4]{3,2,1,0:T(8,128)} copy(s32[1,1,8,4]{2,3,1,0:T(4,128)} %param.9) | data formatting | bytes 256 | tf_op args[1]
  2.0 32.3 %block.1 = (bf16[512,256]{1,0:T(8,128)(2,1)}, f32[8,128]{1,0:T(8,128)}) custom-call(s32[1,1,8,4]{3,2,1,0:T(8,128)} %copy.10.slot_ref, s32[2,2]{1,0:T(2,128)} %shift_ref.1, bf16[1,1,8,4,1024]{4,3,2,1,0:T(4,128)(2,1)} %visible_ref.1, bf16[1024]{0:T(1024)(128)(2,1)} %mask_ref.1, bf16[1024,3072]{1,0:T(8,128)(2,1)} %w_qkv_hbm.1, bf16[1024,1024]{1,0:T(8,128)(2,1)} %w_out_hbm.1, ...), custom_call_target="tpu_custom_call" | custom-call | flops 5905580032 | bytes 16777216 | tf_op jit(solution)/shard_map/block/pallas_call | solution.py:507
  34.3 11.0 %collect.1 = (bf16[8,4,1024]{2,1,0:T(4,128)(2,1)}, f32[1,1024]{1,0:T(1,128)}) custom-call(bf16[16,2,16,256]{3,2,1,0:T(8,128)(2,1)} %bitcast.3, f32[8,128]{1,0:T(8,128)} %get-tuple-element.7.sum_ref), custom_call_target="tpu_custom_call" | custom-call | tf_op jit(solution)/shard_map/collect/pallas_call | solution.py:546
  45.3 1.5 %copy.13 = bf16[1,1,8,4,1024]{4,3,2,1,0:T(4,128)(2,1)} copy(bf16[1,1,8,4,1024]{4,3,2,1,0:T(4,128)(2,1)} %bitcast.4) | data formatting | bytes 131072
  46.8 1.3 %copy.14 = f32[1024]{0:T(1024)} copy(f32[1024]{0:T(1024)} %bitcast.5) | data formatting | bytes 8192
